TPU v7x, 32 devices: a whole 2x2x4 slice. The times are simulated.
32 devices in a mesh: region: 4 (over y, core), sub: 8 (over z, x).
Axes of the slice: x: 2, y: 2, z: 4, core: 2. Of those that a mesh axis runs over, the one named last changes fastest.
Arguments:
- probes: bfloat16 [32, 425984], P(None, ('region', 'sub')), may hold values from -6 to 6
- blocks: bfloat16 [3328, 3, 128, 128], P(('region', 'sub')), may hold values from -0.109375 to 0.109375
- col_slot: int32 [3328, 3], P(('region', 'sub')), may hold values from 0 to 127, as said below
- send_sub: int32 [32, 2, 8], P(('region', 'sub')), may hold values from -1 to 103, as said below
- send_reg: int32 [32, 2, 4], P(('region', 'sub')), may hold values from -1 to 103, as said below
- coeffs: float32 [9], replicated, may hold values from 0.3 to 1
Outputs:
- filtered: float32 [32, 425984], P(None, ('region', 'sub'))
Inputs may be any that keep to these rules, and one draw needn't show every extreme that they name: `col_slot`: entry 0 of each block row names the row's own block. Slots from 104 on name received blocks in this order: 8 from the lower sub neighbour, 8 from the upper sub neighbour, 4 from the lower region neighbour, 4 from the upper one; only received slots that the sender fills are named, and each of those is named by some row. send_sub[d, 0] lists rows sent to sub index one lower in the same region, send_sub[d, 1] to one higher: distinct rows first, then -1; devices at the ends of the sub axis send nothing outward; some list is full. send_reg[d, 0] lists rows sent to the same sub index in the region one lower, send_reg[d, 1] one higher: distinct rows first, then -1; the first and last regions send nothing outward; some list is full.
All inputs are finite; a program needn't handle non-finite values.
Results may differ from a plain program's by a relative error of at most 0.0065.
Values may be sent and summed in bfloat16 or wider, within the bound.
No kernel may reach another device: no remote copies, remote signals or barrier semaphores. Data moves between devices by JAX's collectives and lax.ppermute only.
A program may use at most 128 MiB of HBM per device.

v0:
```python
import functools

import jax
import jax.numpy as jnp
from jax import lax
from jax.experimental import pallas as pl
from jax.experimental.pallas import tpu as pltpu
from jax.sharding import PartitionSpec as P

DEG = 8
BATCH = 8
SMEM = pl.BlockSpec(memory_space=pltpu.SMEM)
VMEM = pl.BlockSpec(memory_space=pltpu.VMEM)
HBM = pl.BlockSpec(memory_space=pl.ANY)
F32, BF16, I32 = jnp.float32, jnp.bfloat16, jnp.int32


def dot(x, b):
    return lax.dot_general(x, b, (((1,), (0,)), ((), ())), preferred_element_type=F32)


def in_vmem(x):
    return pltpu.with_memory_space_constraint(x, pltpu.VMEM)


def divisor(n, most):
    return next(d for d in range(min(n, most), 0, -1) if n % d == 0)


def swaps():
    regions, subs = lax.axis_size("region"), lax.axis_size("sub")

    def route(mate):
        pairs = []
        for r in range(regions):
            for s in range(subs):
                m = mate(r, s)
                if m is not None:
                    pairs.append((r * subs + s, m[0] * subs + m[1]))
        return pairs

    def idle_sub(r, s):
        return (r ^ 1, s) if r ^ 1 < regions else None

    def sub_even(r, s):
        return (r, s ^ 1) if s ^ 1 < subs else idle_sub(r, s)

    def sub_odd(r, s):
        m = ((s - 1) ^ 1) + 1
        return (r, m) if s > 0 and m < subs else idle_sub(r, s)

    def reg_even(r, s):
        return (r ^ 1, s) if r ^ 1 < regions else None

    def reg_odd(r, s):
        m = ((r - 1) ^ 1) + 1
        if r > 0 and m < regions:
            return (m, s)
        return (regions - 1 - r, s) if regions % 2 == 0 else None

    return [route(f) for f in (sub_even, sub_odd, reg_even, reg_odd)]


def exchange(sends):
    routes = swaps()
    order = (0, 1, 3, 2)
    got = [None] * 4
    for i in order:
        got[i] = lax.ppermute(sends[i], ("region", "sub"), routes[i])
    return got


class Layout:
    def __init__(self, rows, hs, hr):
        self.rows, self.hs, self.hr = rows, hs, hr
        self.halo = 2 * hs + 2 * hr
        self.starts = (0, hs, 2 * hs, 2 * hs + hr)
        self.counts = (hs, hs, hr, hr)
        self.loc = 0
        self.far = 3 * rows
        self.tab = self.far + 2 * rows + BATCH
        self.out = self.tab + self.halo
        self.n_far = self.out + 2 * self.halo + BATCH
        self.n_out = self.n_far + 1
        self.size = self.n_out + 1


def pack(place, block, got):
    return place + block * 1024 + got * (1 << 20)


def unpack(code):
    return code & 1023, (code >> 10) & 1023, code >> 20


def send_row(lay, sub_ref, reg_ref, j):
    rp, sp = lax.axis_index("region") % 2, lax.axis_index("sub") % 2
    hs, hr = lay.hs, lay.hr
    if j < hs:
        row = sub_ref[0, 1 - sp, j]
    elif j < 2 * hs:
        row = sub_ref[0, sp, j - hs]
    elif j < 2 * hs + hr:
        row = reg_ref[0, 1 - rp, j - 2 * hs]
    else:
        row = reg_ref[0, rp, j - 2 * hs - hr]
    return jnp.maximum(row, 0)


def first_send_kernel(lay, sub_ref, reg_ref, probes_ref, *send_refs):
    for n, (start, count) in enumerate(zip(lay.starts, lay.counts)):
        for j in range(count):
            row = send_row(lay, sub_ref, reg_ref, start + j)
            send_refs[n][j] = probes_ref[:, pl.ds(pl.multiple_of(row * 128, 128), 128)]


def prologue_kernel(lay, chunk, slot_ref, sub_ref, reg_ref, coeff_ref, probes_ref, blocks_ref,
                    bt_ref, x_ref, y_ref, t_ref, ext_ref, info_ref, raw, sems):
    rows = lay.rows
    chunks = rows // chunk
    copies = [
        pltpu.make_async_copy(blocks_ref.at[pl.ds(c * chunk, chunk)], raw.at[pl.ds(c * chunk, chunk)], sems.at[c])
        for c in range(chunks)
    ]
    for copy in copies:
        copy.start()
    rp, sp = lax.axis_index("region") % 2, lax.axis_index("sub") % 2
    hs, hr = lay.hs, lay.hr

    def received(slot):
        o = slot - rows
        sub_at = jnp.where(sp == 1, o, jnp.where(o < hs, o + hs, o - hs))
        q = o - 2 * hs
        reg_at = jnp.where(rp == 1, o, jnp.where(q < hr, o + hr, o - hr))
        return jnp.where(o < 2 * hs, sub_at, reg_at)

    c0 = coeff_ref[0]
    for i in range(rows):
        v = probes_ref[:, i * 128:(i + 1) * 128]
        ext_ref[i] = v
        x_ref[i] = v.astype(F32)
        t_ref[i] = c0 * v.astype(F32)
    ext_ref[rows] = jnp.zeros_like(ext_ref[rows])
    y_ref[rows] = jnp.zeros_like(y_ref[rows])
    x_ref[rows] = jnp.zeros_like(x_ref[rows])

    def many(c, far):
        pltpu.make_async_copy(blocks_ref.at[pl.ds(c * chunk, chunk)], raw.at[pl.ds(c * chunk, chunk)], sems.at[c]).wait()
        for u in range(chunk):
            i = c * chunk + u
            at = []
            for k in range(3):
                slot = slot_ref[i, k]
                at.append(jnp.where(slot < rows, slot, rows))
                info_ref[lay.loc + 3 * i + k] = at[k]
                if k > 0:
                    info_ref[lay.far + far] = pack(i, 3 * i + k, jnp.maximum(received(slot), 0))
                    far = far + jnp.where(slot < rows, 0, 1)
            turned = [raw[i, k].T for k in range(3)]
            for k in range(3):
                bt_ref[3 * i + k] = turned[k]
            x = jnp.concatenate([ext_ref[at[k]] for k in range(3)], 1)
            y_ref[i] = dot(x, jnp.concatenate(turned, 0))
        return far

    far = lax.fori_loop(0, chunks, many, jnp.int32(0))
    for u in range(BATCH):
        info_ref[lay.far + far + u] = pack(rows, 0, 0)
    info_ref[lay.n_far] = far
    out = jnp.int32(0)
    for j in range(lay.halo):
        row = send_row(lay, sub_ref, reg_ref, j)
        info_ref[lay.tab + j] = row
        for k in (1, 2):
            slot = slot_ref[row, k]
            info_ref[lay.out + out] = pack(j, 3 * row + k, jnp.maximum(received(slot), 0))
            out = out + jnp.where(slot < rows, 0, 1)
    for u in range(BATCH):
        info_ref[lay.out + out + u] = pack(lay.halo, 0, 0)
    info_ref[lay.n_out] = out


def gather_received(lay, got_refs, got):
    for ref, start, count in zip(got_refs, lay.starts, lay.counts):
        for j in range(count):
            got[start + j] = ref[j]


def add_received(factor, info_ref, at, count, bt_ref, got, sum_ref):
    def batch(b, carry):
        found = []
        for u in range(BATCH):
            place, block, source = unpack(info_ref[at + b * BATCH + u])
            found.append((place, dot(got[source], bt_ref[block])))
        for place, value in found:
            sum_ref[place] += factor * value
        return carry

    lax.fori_loop(0, (count + BATCH - 1) // BATCH, batch, 0)


def send_kernel(lay, factor, info_ref, bt_ref, y_ref, g0, g1, g2, g3, y_out, s0, s1, s2, s3, got, held):
    del y_out
    gather_received(lay, (g0, g1, g2, g3), got)
    for j in range(lay.halo):
        held[j] = y_ref[info_ref[lay.tab + j]]
    add_received(factor, info_ref, lay.out, info_ref[lay.n_out], bt_ref, got, held)
    for ref, start, count in zip((s0, s1, s2, s3), lay.starts, lay.counts):
        for j in range(count):
            ref[j] = held[start + j].astype(BF16)


def step_kernel(lay, step, unroll, info_ref, coeff_ref, bt_ref, g0, g1, g2, g3, x_in, y_in, t_in, ext_in,
                x_ref, y_ref, t_ref, ext_ref, got):
    del x_in, y_in, t_in, ext_in
    rows = lay.rows
    factor = 1.0 if step == 1 else 2.0
    gather_received(lay, (g0, g1, g2, g3), got)
    add_received(factor, info_ref, lay.far, info_ref[lay.n_far], bt_ref, got, y_ref)
    for i in range(rows):
        ext_ref[i] = y_ref[i].astype(BF16)
    c = coeff_ref[step]
    last = step == DEG - 1

    def many(j, carry):
        for u in range(unroll):
            i = j * unroll + u
            x = jnp.concatenate([ext_ref[info_ref[lay.loc + 3 * i + k]] for k in range(3)], 1)
            local = dot(x, bt_ref[pl.ds(3 * i, 3)].reshape(3 * 128, 128))
            base = 2.0 * local - x_ref[i]
            if last:
                t_ref[i] += c * y_ref[i] + coeff_ref[DEG] * base
            else:
                t_ref[i] += c * y_ref[i]
                x_ref[i] = base
        return carry

    lax.fori_loop(0, rows // unroll, many, 0)


def final_kernel(lay, info_ref, coeff_ref, bt_ref, t_in, g0, g1, g2, g3, out_ref, t_ref, got):
    del t_in
    gather_received(lay, (g0, g1, g2, g3), got)
    add_received(2.0 * coeff_ref[DEG], info_ref, lay.far, info_ref[lay.n_far], bt_ref, got, t_ref)
    for i in range(lay.rows):
        out_ref[:, i * 128:(i + 1) * 128] = t_ref[i]


def local(probes, blocks, col_slot, send_sub, send_reg, coeffs):
    rows, _, width, _ = blocks.shape
    count = probes.shape[0]
    lay = Layout(rows, send_sub.shape[2], send_reg.shape[2])
    chunk = divisor(rows, 13)
    unroll = divisor(rows, 52)
    small, large = 4 << 20, 20 << 20

    sends_shape = [pltpu.VMEM((n, count, width), BF16) for n in lay.counts]
    got_scratch = pltpu.VMEM((lay.halo, count, width), BF16)
    state = pltpu.VMEM((rows + 1, count, width), F32)

    sends = pl.pallas_call(
        functools.partial(first_send_kernel, lay),
        in_specs=[SMEM, SMEM, VMEM],
        out_specs=[VMEM] * 4,
        out_shape=sends_shape,
        compiler_params=pltpu.CompilerParams(vmem_limit_bytes=small),
        name="first_send",
    )(send_sub, send_reg, probes)
    got = exchange(sends)
    bt, x, y, t, ext, info = pl.pallas_call(
        functools.partial(prologue_kernel, lay, chunk),
        in_specs=[SMEM, SMEM, SMEM, SMEM, VMEM, HBM],
        out_specs=[VMEM] * 5 + [SMEM],
        out_shape=[
            pltpu.VMEM((3 * rows, width, width), BF16),
            state,
            state,
            pltpu.VMEM((rows + 1, count, width), F32),
            pltpu.VMEM((rows + 1, count, width), BF16),
            jax.ShapeDtypeStruct((lay.size,), I32),
        ],
        scratch_shapes=[pltpu.VMEM((rows, 3, width, width), BF16), pltpu.SemaphoreType.DMA((rows // chunk,))],
        compiler_params=pltpu.CompilerParams(vmem_limit_bytes=large),
        name="prologue",
    )(col_slot, send_sub, send_reg, coeffs, probes, pltpu.with_memory_space_constraint(blocks, pltpu.HBM))
    for step in range(1, DEG):
        y, *sends = pl.pallas_call(
            functools.partial(send_kernel, lay, 1.0 if step == 1 else 2.0),
            in_specs=[SMEM, VMEM, VMEM] + [VMEM] * 4,
            out_specs=[VMEM] * 5,
            out_shape=[state] + sends_shape,
            scratch_shapes=[got_scratch, pltpu.VMEM((lay.halo + 1, count, width), F32)],
            input_output_aliases={2: 0},
            compiler_params=pltpu.CompilerParams(vmem_limit_bytes=small),
            name="send",
        )(info, in_vmem(bt), in_vmem(y), *[in_vmem(g) for g in got])
        later = exchange(sends)
        x, y, t, ext = pl.pallas_call(
            functools.partial(step_kernel, lay, step, unroll),
            in_specs=[SMEM, SMEM, VMEM] + [VMEM] * 8,
            out_specs=[VMEM] * 4,
            out_shape=[state, state, state, pltpu.VMEM((rows + 1, count, width), BF16)],
            scratch_shapes=[got_scratch],
            input_output_aliases={7: 0, 8: 1, 9: 2, 10: 3},
            compiler_params=pltpu.CompilerParams(vmem_limit_bytes=small),
            cost_estimate=pl.CostEstimate(flops=2 * rows * 3 * width * width * count, bytes_accessed=1 << 20, transcendentals=0),
            name="step",
        )(info, coeffs, in_vmem(bt), *[in_vmem(g) for g in got], in_vmem(x), in_vmem(y), in_vmem(t), in_vmem(ext))
        x, y = y, x
        got = later
    out, _ = pl.pallas_call(
        functools.partial(final_kernel, lay),
        in_specs=[SMEM, SMEM, VMEM, VMEM] + [VMEM] * 4,
        out_specs=[VMEM, VMEM],
        out_shape=[jax.ShapeDtypeStruct((count, rows * width), F32), state],
        scratch_shapes=[got_scratch],
        input_output_aliases={3: 1},
        compiler_params=pltpu.CompilerParams(vmem_limit_bytes=small),
        name="final",
    )(info, coeffs, in_vmem(bt), in_vmem(t), *[in_vmem(g) for g in got])
    return out


def solution(mesh):
    return jax.shard_map(
        local,
        mesh=mesh,
        in_specs=(
            P(None, ("region", "sub")),
            P(("region", "sub"), None, None, None),
            P(("region", "sub"), None),
            P(("region", "sub"), None, None),
            P(("region", "sub"), None, None),
            P(),
        ),
        out_specs=P(None, ("region", "sub")),
        check_vma=False,
    )
```

profile of v0, /device:TPU:1, one launch (start us, length us, event | category | flops | bytes accessed | tf_op | source)
XLA Modules:
  0.0 76.3 jit_solution(8465792206792896365)
XLA Ops:
  0.0 1.2 %copy-done = bf16[32,13312]{1,0:T(8,128)(2,1)S(1)} copy-done((bf16[32,13312]{1,0:T(8,128)(2,1)S(1)}, bf16[32,13312]{1,0:T(8,128)(2,1)}, u32[]{:S(2)}) %copy-start) | copy-done | bytes 851992
  3.2 2.1 %collective-permute-start = (bf16[8,32,128]{2,1,0:T(8,128)(2,1)S(1)}, bf16[8,32,128]{2,1,0:T(8,128)(2,1)S(1)}, u32[]{:S(2)}, u32[]{:S(2)}) collective-permute-start(bf16[8,32,128]{2,1,0:T(8,128)(2,1)S(1)} %get-tuple-element.78), channel_id=1, source_target_pairs={{0,1},{1,0},{2,3},{3,2},{4,5},{5,4},{6,7},{7,6},{8,9},{9,8},{10,11... | collective-permute-start | bytes 196616 | tf_op jit(solution)/shard_map/ppermute | solution.py:69
  6.2 1.6 %collective-permute-start.3 = (bf16[4,32,128]{2,1,0:T(8,128)(2,1)S(1)}, bf16[4,32,128]{2,1,0:T(8,128)(2,1)S(1)}, u32[]{:S(2)}, u32[]{:S(2)}) collective-permute-start(bf16[4,32,128]{2,1,0:T(8,128)(2,1)S(1)} %get-tuple-element.81), channel_id=1, source_target_pairs={{0,24},{1,25},{2,26},{3,27},{4,28},{5,29},{6,30},{7,31},{8,16},{9,... | collective-permute-start | bytes 98312 | tf_op jit(solution)/shard_map/ppermute | solution.py:69
  8.6 1.1 %copy-done.1 = bf16[32,13312]{1,0:T(8,128)(2,1)S(1)} copy-done((bf16[32,13312]{1,0:T(8,128)(2,1)S(1)}, bf16[32,13312]{1,0:T(8,128)(2,1)}, u32[]{:S(2)}) %copy-start.1) | copy-done | bytes 851992
  11.8 8.0 %prologue.1 = (bf16[312,128,128]{2,1,0:T(8,128)(2,1)S(1)}, f32[105,32,128]{2,1,0:T(8,128)S(1)}, f32[105,32,128]{2,1,0:T(8,128)S(1)}, f32[105,32,128]{2,1,0:T(8,1...) custom-call(s32[104,3]{1,0:T(8,128)S(1)} %copy.43.slot_ref, s32[1,2,8]{2,1,0:T(2,128)S(1)} %copy-done.5, ...), custom_call_target="tpu_custom_call" | custom-call | tf_op jit(solution)/shard_map/prologue/pallas_call | solution.py:270
  20.7 2.3 %collective-permute-start.4 = (bf16[8,32,128]{2,1,0:T(8,128)(2,1)S(1)}, bf16[8,32,128]{2,1,0:T(8,128)(2,1)S(1)}, u32[]{:S(2)}, u32[]{:S(2)}) collective-permute-start(bf16[8,32,128]{2,1,0:T(8,128)(2,1)S(1)} %get-tuple-element.88), channel_id=1, source_target_pairs={{0,1},{1,0},{2,3},{3,2},{4,5},{5,4},{6,7},{7,6},{8,9},{9,8},{10,11... | collective-permute-start | bytes 196616 | tf_op jit(solution)/shard_map/ppermute | solution.py:69
  24.6 3.1 %step.7 = (f32[105,32,128]{2,1,0:T(8,128)S(1)}, f32[105,32,128]{2,1,0:T(8,128)S(1)}, f32[105,32,128]{2,1,0:T(8,128)S(1)}, bf16[105,32,128]{2,1,0:T(8,128)(2,1)S(1)}) custom-call(s32[610]{0:T(1024)S(1)} %get-tuple-element.76.info_ref, f32[9]{0:T(128)S(1)} %copy-done.2, ...), custom_call_target="tpu_custom_call", output_to_operand_aliasing={{0}: (7, {}), {1}: (8, {}), {2}: (9, {}), {3}: (10, {})} | custom-call | flops 327155712 | bytes 1048576 | tf_op jit(solution)/shard_map/step/pallas_call | solution.py:298
  28.6 2.2 %collective-permute-start.8 = (bf16[8,32,128]{2,1,0:T(8,128)(2,1)S(1)}, bf16[8,32,128]{2,1,0:T(8,128)(2,1)S(1)}, u32[]{:S(2)}, u32[]{:S(2)}) collective-permute-start(bf16[8,32,128]{2,1,0:T(8,128)(2,1)S(1)} %get-tuple-element.92), channel_id=1, source_target_pairs={{0,1},{1,0},{2,3},{3,2},{4,5},{5,4},{6,7},{7,6},{8,9},{9,8},{10,11... | collective-permute-start | bytes 196616 | tf_op jit(solution)/shard_map/ppermute | solution.py:69
  31.7 1.8 %collective-permute-start.11 = (bf16[4,32,128]{2,1,0:T(8,128)(2,1)S(1)}, bf16[4,32,128]{2,1,0:T(8,128)(2,1)S(1)}, u32[]{:S(2)}, u32[]{:S(2)}) collective-permute-start(bf16[4,32,128]{2,1,0:T(8,128)(2,1)S(1)} %get-tuple-element.95), channel_id=1, source_target_pairs={{0,24},{1,25},{2,26},{3,27},{4,28},{5,29},{6,30},{7,31},{8,16},{9,... | collective-permute-start | bytes 98312 | tf_op jit(solution)/shard_map/ppermute | solution.py:69
  33.5 3.1 %step.8 = (f32[105,32,128]{2,1,0:T(8,128)S(1)}, f32[105,32,128]{2,1,0:T(8,128)S(1)}, f32[105,32,128]{2,1,0:T(8,128)S(1)}, bf16[105,32,128]{2,1,0:T(8,128)(2,1)S(1)}) custom-call(s32[610]{0:T(1024)S(1)} %get-tuple-element.76.info_ref, f32[9]{0:T(128)S(1)} %copy-done.3, ...), custom_call_target="tpu_custom_call", output_to_operand_aliasing={{0}: (7, {}), {1}: (8, {}), {2}: (9, {}), {3}: (10, {})} | custom-call | flops 327155712 | bytes 1048576 | tf_op jit(solution)/shard_map/step/pallas_call | solution.py:298
  37.5 1.9 %collective-permute-start.12 = (bf16[8,32,128]{2,1,0:T(8,128)(2,1)S(1)}, bf16[8,32,128]{2,1,0:T(8,128)(2,1)S(1)}, u32[]{:S(2)}, u32[]{:S(2)}) collective-permute-start(bf16[8,32,128]{2,1,0:T(8,128)(2,1)S(1)} %get-tuple-element.106), channel_id=1, source_target_pairs={{0,1},{1,0},{2,3},{3,2},{4,5},{5,4},{6,7},{7,6},{8,9},{9,8},{10,11... | collective-permute-start | bytes 196616 | tf_op jit(solution)/shard_map/ppermute | solution.py:69
  39.4 1.0 %collective-permute-start.13 = (bf16[8,32,128]{2,1,0:T(8,128)(2,1)S(1)}, bf16[8,32,128]{2,1,0:T(8,128)(2,1)S(1)}, u32[]{:S(2)}, u32[]{:S(2)}) collective-permute-start(bf16[8,32,128]{2,1,0:T(8,128)(2,1)S(1)} %get-tuple-element.107), channel_id=1, source_target_pairs={{0,8},{1,2},{2,1},{3,4},{4,3},{5,6},{6,5},{7,15},{8,0},{9,10},{10,... | collective-permute-start | bytes 196616 | tf_op jit(solution)/shard_map/ppermute | solution.py:69
  41.2 3.1 %step.9 = (f32[105,32,128]{2,1,0:T(8,128)S(1)}, f32[105,32,128]{2,1,0:T(8,128)S(1)}, f32[105,32,128]{2,1,0:T(8,128)S(1)}, bf16[105,32,128]{2,1,0:T(8,128)(2,1)S(1)}) custom-call(s32[610]{0:T(1024)S(1)} %get-tuple-element.76.info_ref, f32[9]{0:T(128)S(1)} %copy-done.3, ...), custom_call_target="tpu_custom_call", output_to_operand_aliasing={{0}: (7, {}), {1}: (8, {}), {2}: (9, {}), {3}: (10, {})} | custom-call | flops 327155712 | bytes 1048576 | tf_op jit(solution)/shard_map/step/pallas_call | solution.py:298
  47.8 3.1 %step.10 = (f32[105,32,128]{2,1,0:T(8,128)S(1)}, f32[105,32,128]{2,1,0:T(8,128)S(1)}, f32[105,32,128]{2,1,0:T(8,128)S(1)}, bf16[105,32,128]{2,1,0:T(8,128)(2,1)S(1)}) custom-call(s32[610]{0:T(1024)S(1)} %get-tuple-element.76.info_ref, f32[9]{0:T(128)S(1)} %copy-done.3, ...), custom_call_target="tpu_custom_call", output_to_operand_aliasing={{0}: (7, {}), {1}: (8, {}), {2}: (9, {}), {3}: (10, {})} | custom-call | flops 327155712 | bytes 1048576 | tf_op jit(solution)/shard_map/step/pallas_call | solution.py:298
  51.8 1.6 %collective-permute-start.20 = (bf16[8,32,128]{2,1,0:T(8,128)(2,1)S(1)}, bf16[8,32,128]{2,1,0:T(8,128)(2,1)S(1)}, u32[]{:S(2)}, u32[]{:S(2)}) collective-permute-start(bf16[8,32,128]{2,1,0:T(8,128)(2,1)S(1)} %get-tuple-element.124), channel_id=1, source_target_pairs={{0,1},{1,0},{2,3},{3,2},{4,5},{5,4},{6,7},{7,6},{8,9},{9,8},{10,11... | collective-permute-start | bytes 196616 | tf_op jit(solution)/shard_map/ppermute | solution.py:69
  54.4 1.0 %collective-permute-start.23 = (bf16[4,32,128]{2,1,0:T(8,128)(2,1)S(1)}, bf16[4,32,128]{2,1,0:T(8,128)(2,1)S(1)}, u32[]{:S(2)}, u32[]{:S(2)}) collective-permute-start(bf16[4,32,128]{2,1,0:T(8,128)(2,1)S(1)} %get-tuple-element.127), channel_id=1, source_target_pairs={{0,24},{1,25},{2,26},{3,27},{4,28},{5,29},{6,30},{7,31},{8,16},{9,... | collective-permute-start | bytes 98312 | tf_op jit(solution)/shard_map/ppermute | solution.py:69
  55.4 3.1 %step.11 = (f32[105,32,128]{2,1,0:T(8,128)S(1)}, f32[105,32,128]{2,1,0:T(8,128)S(1)}, f32[105,32,128]{2,1,0:T(8,128)S(1)}, bf16[105,32,128]{2,1,0:T(8,128)(2,1)S(1)}) custom-call(s32[610]{0:T(1024)S(1)} %get-tuple-element.76.info_ref, f32[9]{0:T(128)S(1)} %copy-done.3, ...), custom_call_target="tpu_custom_call", output_to_operand_aliasing={{0}: (7, {}), {1}: (8, {}), {2}: (9, {}), {3}: (10, {})} | custom-call | flops 327155712 | bytes 1048576 | tf_op jit(solution)/shard_map/step/pallas_call | solution.py:298
  59.4 1.5 %collective-permute-start.24 = (bf16[8,32,128]{2,1,0:T(8,128)(2,1)S(1)}, bf16[8,32,128]{2,1,0:T(8,128)(2,1)S(1)}, u32[]{:S(2)}, u32[]{:S(2)}) collective-permute-start(bf16[8,32,128]{2,1,0:T(8,128)(2,1)S(1)} %get-tuple-element.128), channel_id=1, source_target_pairs={{0,1},{1,0},{2,3},{3,2},{4,5},{5,4},{6,7},{7,6},{8,9},{9,8},{10,11... | collective-permute-start | bytes 196616 | tf_op jit(solution)/shard_map/ppermute | solution.py:69
  61.9 1.2 %collective-permute-start.27 = (bf16[4,32,128]{2,1,0:T(8,128)(2,1)S(1)}, bf16[4,32,128]{2,1,0:T(8,128)(2,1)S(1)}, u32[]{:S(2)}, u32[]{:S(2)}) collective-permute-start(bf16[4,32,128]{2,1,0:T(8,128)(2,1)S(1)} %get-tuple-element.131), channel_id=1, source_target_pairs={{0,24},{1,25},{2,26},{3,27},{4,28},{5,29},{6,30},{7,31},{8,16},{9,... | collective-permute-start | bytes 98312 | tf_op jit(solution)/shard_map/ppermute | solution.py:69
  63.0 3.3 %step.12 = (f32[105,32,128]{2,1,0:T(8,128)S(1)}, f32[105,32,128]{2,1,0:T(8,128)S(1)}, f32[105,32,128]{2,1,0:T(8,128)S(1)}, bf16[105,32,128]{2,1,0:T(8,128)(2,1)S(1)}) custom-call(s32[610]{0:T(1024)S(1)} %get-tuple-element.76.info_ref, f32[9]{0:T(128)S(1)} %copy-done.3, ...), custom_call_target="tpu_custom_call", output_to_operand_aliasing={{0}: (7, {}), {1}: (8, {}), {2}: (9, {}), {3}: (10, {})} | custom-call | flops 327155712 | bytes 1048576 | tf_op jit(solution)/shard_map/step/pallas_call | solution.py:298
  67.2 1.5 %collective-permute-start.28 = (bf16[8,32,128]{2,1,0:T(8,128)(2,1)S(1)}, bf16[8,32,128]{2,1,0:T(8,128)(2,1)S(1)}, u32[]{:S(2)}, u32[]{:S(2)}) collective-permute-start(bf16[8,32,128]{2,1,0:T(8,128)(2,1)S(1)} %get-tuple-element.142), channel_id=1, source_target_pairs={{0,1},{1,0},{2,3},{3,2},{4,5},{5,4},{6,7},{7,6},{8,9},{9,8},{10,11... | collective-permute-start | bytes 196616 | tf_op jit(solution)/shard_map/ppermute | solution.py:69
  69.7 1.2 %collective-permute-start.31 = (bf16[4,32,128]{2,1,0:T(8,128)(2,1)S(1)}, bf16[4,32,128]{2,1,0:T(8,128)(2,1)S(1)}, u32[]{:S(2)}, u32[]{:S(2)}) collective-permute-start(bf16[4,32,128]{2,1,0:T(8,128)(2,1)S(1)} %get-tuple-element.145), channel_id=1, source_target_pairs={{0,24},{1,25},{2,26},{3,27},{4,28},{5,29},{6,30},{7,31},{8,16},{9,... | collective-permute-start | bytes 98312 | tf_op jit(solution)/shard_map/ppermute | solution.py:69
  70.9 3.1 %step.13 = (f32[105,32,128]{2,1,0:T(8,128)S(1)}, f32[105,32,128]{2,1,0:T(8,128)S(1)}, f32[105,32,128]{2,1,0:T(8,128)S(1)}, bf16[105,32,128]{2,1,0:T(8,128)(2,1)S(1)}) custom-call(s32[610]{0:T(1024)S(1)} %get-tuple-element.76.info_ref, f32[9]{0:T(128)S(1)} %copy-done.3, ...), custom_call_target="tpu_custom_call", output_to_operand_aliasing={{0}: (7, {}), {1}: (8, {}), {2}: (9, {}), {3}: (10, {})} | custom-call | flops 327155712 | bytes 1048576 | tf_op jit(solution)/shard_map/step/pallas_call | solution.py:298
  74.0 2.3 %final.1 = (f32[32,13312]{1,0:T(8,128)}, f32[105,32,128]{2,1,0:T(8,128)S(1)}) custom-call(s32[610]{0:T(1024)S(1)} %get-tuple-element.76.info_ref, f32[9]{0:T(128)S(1)} %copy-done.3, bf16[312,128,128]{2,1,0:T(8,128)(2,1)S(1)} %get-tuple-element.77.bt_ref, f32[105,32,128]{2,1,0:T(8,128)S(1)} %get-tuple-element.141.t_in, ...), custom_call_target="tpu_custom_call", output_to_operand_aliasing={{1}: (3, {})} | custom-call | tf_op jit(solution)/shard_map/final/pallas_call | solution.py:311
  (74 shorter events, 20.5 us)
Async XLA Ops:
  3.2 16.7 %collective-permute-start = (bf16[8,32,128]{2,1,0:T(8,128)(2,1)S(1)}, bf16[8,32,128]{2,1,0:T(8,128)(2,1)S(1)}, u32[]{:S(2)}, u32[]{:S(2)}) collective-permute-start(bf16[8,32,128]{2,1,0:T(8,128)(2,1)S(1)} %get-tuple-element.78), channel_id=1, source_target_pairs={{0,1},{1,0},{2,3},{3,2},{4,5},{5,4},{6,7},{7,6},{8,9},{9,8},{10,11... | collective-permute-start | bytes 196616 | tf_op jit(solution)/shard_map/ppermute | solution.py:69
  5.3 14.6 %collective-permute-start.1 = (bf16[8,32,128]{2,1,0:T(8,128)(2,1)S(1)}, bf16[8,32,128]{2,1,0:T(8,128)(2,1)S(1)}, u32[]{:S(2)}, u32[]{:S(2)}) collective-permute-start(bf16[8,32,128]{2,1,0:T(8,128)(2,1)S(1)} %get-tuple-element.79), channel_id=1, source_target_pairs={{0,8},{1,2},{2,1},{3,4},{4,3},{5,6},{6,5},{7,15},{8,0},{9,10},{10,... | collective-permute-start | bytes 196616 | tf_op jit(solution)/shard_map/ppermute | solution.py:69
  6.2 13.6 %collective-permute-start.2 = (bf16[4,32,128]{2,1,0:T(8,128)(2,1)S(1)}, bf16[4,32,128]{2,1,0:T(8,128)(2,1)S(1)}, u32[]{:S(2)}, u32[]{:S(2)}) collective-permute-start(bf16[4,32,128]{2,1,0:T(8,128)(2,1)S(1)} %get-tuple-element.80), channel_id=1, source_target_pairs={{0,8},{1,9},{2,10},{3,11},{4,12},{5,13},{6,14},{7,15},{8,0},{9,1},... | collective-permute-start | bytes 98312 | tf_op jit(solution)/shard_map/ppermute | solution.py:69
  6.2 13.6 %collective-permute-start.3 = (bf16[4,32,128]{2,1,0:T(8,128)(2,1)S(1)}, bf16[4,32,128]{2,1,0:T(8,128)(2,1)S(1)}, u32[]{:S(2)}, u32[]{:S(2)}) collective-permute-start(bf16[4,32,128]{2,1,0:T(8,128)(2,1)S(1)} %get-tuple-element.81), channel_id=1, source_target_pairs={{0,24},{1,25},{2,26},{3,27},{4,28},{5,29},{6,30},{7,31},{8,16},{9,... | collective-permute-start | bytes 98312 | tf_op jit(solution)/shard_map/ppermute | solution.py:69
  20.7 7.0 %collective-permute-start.4 = (bf16[8,32,128]{2,1,0:T(8,128)(2,1)S(1)}, bf16[8,32,128]{2,1,0:T(8,128)(2,1)S(1)}, u32[]{:S(2)}, u32[]{:S(2)}) collective-permute-start(bf16[8,32,128]{2,1,0:T(8,128)(2,1)S(1)} %get-tuple-element.88), channel_id=1, source_target_pairs={{0,1},{1,0},{2,3},{3,2},{4,5},{5,4},{6,7},{7,6},{8,9},{9,8},{10,11... | collective-permute-start | bytes 196616 | tf_op jit(solution)/shard_map/ppermute | solution.py:69
  23.0 4.7 %collective-permute-start.5 = (bf16[8,32,128]{2,1,0:T(8,128)(2,1)S(1)}, bf16[8,32,128]{2,1,0:T(8,128)(2,1)S(1)}, u32[]{:S(2)}, u32[]{:S(2)}) collective-permute-start(bf16[8,32,128]{2,1,0:T(8,128)(2,1)S(1)} %get-tuple-element.89), channel_id=1, source_target_pairs={{0,8},{1,2},{2,1},{3,4},{4,3},{5,6},{6,5},{7,15},{8,0},{9,10},{10,... | collective-permute-start | bytes 196616 | tf_op jit(solution)/shard_map/ppermute | solution.py:69
  28.6 8.1 %collective-permute-start.8 = (bf16[8,32,128]{2,1,0:T(8,128)(2,1)S(1)}, bf16[8,32,128]{2,1,0:T(8,128)(2,1)S(1)}, u32[]{:S(2)}, u32[]{:S(2)}) collective-permute-start(bf16[8,32,128]{2,1,0:T(8,128)(2,1)S(1)} %get-tuple-element.92), channel_id=1, source_target_pairs={{0,1},{1,0},{2,3},{3,2},{4,5},{5,4},{6,7},{7,6},{8,9},{9,8},{10,11... | collective-permute-start | bytes 196616 | tf_op jit(solution)/shard_map/ppermute | solution.py:69
  30.8 5.8 %collective-permute-start.9 = (bf16[8,32,128]{2,1,0:T(8,128)(2,1)S(1)}, bf16[8,32,128]{2,1,0:T(8,128)(2,1)S(1)}, u32[]{:S(2)}, u32[]{:S(2)}) collective-permute-start(bf16[8,32,128]{2,1,0:T(8,128)(2,1)S(1)} %get-tuple-element.93), channel_id=1, source_target_pairs={{0,8},{1,2},{2,1},{3,4},{4,3},{5,6},{6,5},{7,15},{8,0},{9,10},{10,... | collective-permute-start | bytes 196616 | tf_op jit(solution)/shard_map/ppermute | solution.py:69
  31.7 4.9 %collective-permute-start.10 = (bf16[4,32,128]{2,1,0:T(8,128)(2,1)S(1)}, bf16[4,32,128]{2,1,0:T(8,128)(2,1)S(1)}, u32[]{:S(2)}, u32[]{:S(2)}) collective-permute-start(bf16[4,32,128]{2,1,0:T(8,128)(2,1)S(1)} %get-tuple-element.94), channel_id=1, source_target_pairs={{0,8},{1,9},{2,10},{3,11},{4,12},{5,13},{6,14},{7,15},{8,0},{9,1},... | collective-permute-start | bytes 98312 | tf_op jit(solution)/shard_map/ppermute | solution.py:69
  31.7 4.9 %collective-permute-start.11 = (bf16[4,32,128]{2,1,0:T(8,128)(2,1)S(1)}, bf16[4,32,128]{2,1,0:T(8,128)(2,1)S(1)}, u32[]{:S(2)}, u32[]{:S(2)}) collective-permute-start(bf16[4,32,128]{2,1,0:T(8,128)(2,1)S(1)} %get-tuple-element.95), channel_id=1, source_target_pairs={{0,24},{1,25},{2,26},{3,27},{4,28},{5,29},{6,30},{7,31},{8,16},{9,... | collective-permute-start | bytes 98312 | tf_op jit(solution)/shard_map/ppermute | solution.py:69
  37.5 6.8 %collective-permute-start.12 = (bf16[8,32,128]{2,1,0:T(8,128)(2,1)S(1)}, bf16[8,32,128]{2,1,0:T(8,128)(2,1)S(1)}, u32[]{:S(2)}, u32[]{:S(2)}) collective-permute-start(bf16[8,32,128]{2,1,0:T(8,128)(2,1)S(1)} %get-tuple-element.106), channel_id=1, source_target_pairs={{0,1},{1,0},{2,3},{3,2},{4,5},{5,4},{6,7},{7,6},{8,9},{9,8},{10,11... | collective-permute-start | bytes 196616 | tf_op jit(solution)/shard_map/ppermute | solution.py:69
  39.4 4.9 %collective-permute-start.13 = (bf16[8,32,128]{2,1,0:T(8,128)(2,1)S(1)}, bf16[8,32,128]{2,1,0:T(8,128)(2,1)S(1)}, u32[]{:S(2)}, u32[]{:S(2)}) collective-permute-start(bf16[8,32,128]{2,1,0:T(8,128)(2,1)S(1)} %get-tuple-element.107), channel_id=1, source_target_pairs={{0,8},{1,2},{2,1},{3,4},{4,3},{5,6},{6,5},{7,15},{8,0},{9,10},{10,... | collective-permute-start | bytes 196616 | tf_op jit(solution)/shard_map/ppermute | solution.py:69
  45.2 5.7 %collective-permute-start.16 = (bf16[8,32,128]{2,1,0:T(8,128)(2,1)S(1)}, bf16[8,32,128]{2,1,0:T(8,128)(2,1)S(1)}, u32[]{:S(2)}, u32[]{:S(2)}) collective-permute-start(bf16[8,32,128]{2,1,0:T(8,128)(2,1)S(1)} %get-tuple-element.110), channel_id=1, source_target_pairs={{0,1},{1,0},{2,3},{3,2},{4,5},{5,4},{6,7},{7,6},{8,9},{9,8},{10,11... | collective-permute-start | bytes 196616 | tf_op jit(solution)/shard_map/ppermute | solution.py:69
  46.0 4.9 %collective-permute-start.17 = (bf16[8,32,128]{2,1,0:T(8,128)(2,1)S(1)}, bf16[8,32,128]{2,1,0:T(8,128)(2,1)S(1)}, u32[]{:S(2)}, u32[]{:S(2)}) collective-permute-start(bf16[8,32,128]{2,1,0:T(8,128)(2,1)S(1)} %get-tuple-element.111), channel_id=1, source_target_pairs={{0,8},{1,2},{2,1},{3,4},{4,3},{5,6},{6,5},{7,15},{8,0},{9,10},{10,... | collective-permute-start | bytes 196616 | tf_op jit(solution)/shard_map/ppermute | solution.py:69
  51.8 6.7 %collective-permute-start.20 = (bf16[8,32,128]{2,1,0:T(8,128)(2,1)S(1)}, bf16[8,32,128]{2,1,0:T(8,128)(2,1)S(1)}, u32[]{:S(2)}, u32[]{:S(2)}) collective-permute-start(bf16[8,32,128]{2,1,0:T(8,128)(2,1)S(1)} %get-tuple-element.124), channel_id=1, source_target_pairs={{0,1},{1,0},{2,3},{3,2},{4,5},{5,4},{6,7},{7,6},{8,9},{9,8},{10,11... | collective-permute-start | bytes 196616 | tf_op jit(solution)/shard_map/ppermute | solution.py:69
  53.4 5.1 %collective-permute-start.21 = (bf16[8,32,128]{2,1,0:T(8,128)(2,1)S(1)}, bf16[8,32,128]{2,1,0:T(8,128)(2,1)S(1)}, u32[]{:S(2)}, u32[]{:S(2)}) collective-permute-start(bf16[8,32,128]{2,1,0:T(8,128)(2,1)S(1)} %get-tuple-element.125), channel_id=1, source_target_pairs={{0,8},{1,2},{2,1},{3,4},{4,3},{5,6},{6,5},{7,15},{8,0},{9,10},{10,... | collective-permute-start | bytes 196616 | tf_op jit(solution)/shard_map/ppermute | solution.py:69
  59.4 7.0 %collective-permute-start.24 = (bf16[8,32,128]{2,1,0:T(8,128)(2,1)S(1)}, bf16[8,32,128]{2,1,0:T(8,128)(2,1)S(1)}, u32[]{:S(2)}, u32[]{:S(2)}) collective-permute-start(bf16[8,32,128]{2,1,0:T(8,128)(2,1)S(1)} %get-tuple-element.128), channel_id=1, source_target_pairs={{0,1},{1,0},{2,3},{3,2},{4,5},{5,4},{6,7},{7,6},{8,9},{9,8},{10,11... | collective-permute-start | bytes 196616 | tf_op jit(solution)/shard_map/ppermute | solution.py:69
  60.9 5.5 %collective-permute-start.25 = (bf16[8,32,128]{2,1,0:T(8,128)(2,1)S(1)}, bf16[8,32,128]{2,1,0:T(8,128)(2,1)S(1)}, u32[]{:S(2)}, u32[]{:S(2)}) collective-permute-start(bf16[8,32,128]{2,1,0:T(8,128)(2,1)S(1)} %get-tuple-element.129), channel_id=1, source_target_pairs={{0,8},{1,2},{2,1},{3,4},{4,3},{5,6},{6,5},{7,15},{8,0},{9,10},{10,... | collective-permute-start | bytes 196616 | tf_op jit(solution)/shard_map/ppermute | solution.py:69
  61.9 4.5 %collective-permute-start.26 = (bf16[4,32,128]{2,1,0:T(8,128)(2,1)S(1)}, bf16[4,32,128]{2,1,0:T(8,128)(2,1)S(1)}, u32[]{:S(2)}, u32[]{:S(2)}) collective-permute-start(bf16[4,32,128]{2,1,0:T(8,128)(2,1)S(1)} %get-tuple-element.130), channel_id=1, source_target_pairs={{0,8},{1,9},{2,10},{3,11},{4,12},{5,13},{6,14},{7,15},{8,0},{9,1},... | collective-permute-start | bytes 98312 | tf_op jit(solution)/shard_map/ppermute | solution.py:69
  61.9 4.5 %collective-permute-start.27 = (bf16[4,32,128]{2,1,0:T(8,128)(2,1)S(1)}, bf16[4,32,128]{2,1,0:T(8,128)(2,1)S(1)}, u32[]{:S(2)}, u32[]{:S(2)}) collective-permute-start(bf16[4,32,128]{2,1,0:T(8,128)(2,1)S(1)} %get-tuple-element.131), channel_id=1, source_target_pairs={{0,24},{1,25},{2,26},{3,27},{4,28},{5,29},{6,30},{7,31},{8,16},{9,... | collective-permute-start | bytes 98312 | tf_op jit(solution)/shard_map/ppermute | solution.py:69
  67.2 6.8 %collective-permute-start.28 = (bf16[8,32,128]{2,1,0:T(8,128)(2,1)S(1)}, bf16[8,32,128]{2,1,0:T(8,128)(2,1)S(1)}, u32[]{:S(2)}, u32[]{:S(2)}) collective-permute-start(bf16[8,32,128]{2,1,0:T(8,128)(2,1)S(1)} %get-tuple-element.142), channel_id=1, source_target_pairs={{0,1},{1,0},{2,3},{3,2},{4,5},{5,4},{6,7},{7,6},{8,9},{9,8},{10,11... | collective-permute-start | bytes 196616 | tf_op jit(solution)/shard_map/ppermute | solution.py:69
  68.7 5.3 %collective-permute-start.29 = (bf16[8,32,128]{2,1,0:T(8,128)(2,1)S(1)}, bf16[8,32,128]{2,1,0:T(8,128)(2,1)S(1)}, u32[]{:S(2)}, u32[]{:S(2)}) collective-permute-start(bf16[8,32,128]{2,1,0:T(8,128)(2,1)S(1)} %get-tuple-element.143), channel_id=1, source_target_pairs={{0,8},{1,2},{2,1},{3,4},{4,3},{5,6},{6,5},{7,15},{8,0},{9,10},{10,... | collective-permute-start | bytes 196616 | tf_op jit(solution)/shard_map/ppermute | solution.py:69
  69.7 4.3 %collective-permute-start.30 = (bf16[4,32,128]{2,1,0:T(8,128)(2,1)S(1)}, bf16[4,32,128]{2,1,0:T(8,128)(2,1)S(1)}, u32[]{:S(2)}, u32[]{:S(2)}) collective-permute-start(bf16[4,32,128]{2,1,0:T(8,128)(2,1)S(1)} %get-tuple-element.144), channel_id=1, source_target_pairs={{0,8},{1,9},{2,10},{3,11},{4,12},{5,13},{6,14},{7,15},{8,0},{9,1},... | collective-permute-start | bytes 98312 | tf_op jit(solution)/shard_map/ppermute | solution.py:69
  69.7 4.3 %collective-permute-start.31 = (bf16[4,32,128]{2,1,0:T(8,128)(2,1)S(1)}, bf16[4,32,128]{2,1,0:T(8,128)(2,1)S(1)}, u32[]{:S(2)}, u32[]{:S(2)}) collective-permute-start(bf16[4,32,128]{2,1,0:T(8,128)(2,1)S(1)} %get-tuple-element.145), channel_id=1, source_target_pairs={{0,24},{1,25},{2,26},{3,27},{4,28},{5,29},{6,30},{7,31},{8,16},{9,... | collective-permute-start | bytes 98312 | tf_op jit(solution)/shard_map/ppermute | solution.py:69
  (16 other events, 43.2 us)
where the time goes:
time: 77.1 us; the launch traced here: 76.3 us
  Pallas kernels  38.6 us (50%)
  starting transfers between devices  30.8 us (40%)
  local copies, waits for them, and re-layouts  6.46 us (8%)
    ppermute x32, starting transfers between devices, exchange(): got[i] = lax.ppermute(sends[i], ('region', 'sub'), routes[i])  30.8 us
    pallas_call x7, Pallas kernels, local(): pl.pallas_call(functools.partial(step_kernel, lay, step, unroll), in_spec...  21.8 us
    pallas_call x1, Pallas kernels, local(): pl.pallas_call(functools.partial(prologue_kernel, lay, chunk), in_specs=[...  7.97 us
    unnamed x17, local copies, waits for them, and re-layouts  6.46 us
    pallas_call x7, Pallas kernels, local(): pl.pallas_call(functools.partial(send_kernel, lay, 1.0 if step == 1 else...  5.85 us
    pallas_call x1, Pallas kernels, local(): pl.pallas_call(functools.partial(final_kernel, lay), in_specs=[SMEM, SMEM...  2.28 us
  transfers between devices with their start and end apart: 32, of which 0 were waited for; matrix products, arithmetic and copies ran while one was open for 1% of the time, Pallas kernels for 39%

commit v1 on v0

--- a/solution.py
+++ b/solution.py
@@ -8,7 +8,9 @@
 from jax.sharding import PartitionSpec as P
 
 DEG = 8
-BATCH = 8
+BATCH = 16
+FIRST = 13
+ORDER = (0, 1, 3, 2)
 SMEM = pl.BlockSpec(memory_space=pltpu.SMEM)
 VMEM = pl.BlockSpec(memory_space=pltpu.VMEM)
 HBM = pl.BlockSpec(memory_space=pl.ANY)
@@ -21,6 +23,14 @@
 
 def in_vmem(x):
     return pltpu.with_memory_space_constraint(x, pltpu.VMEM)
+
+
+def in_hbm(x):
+    return pltpu.with_memory_space_constraint(x, pltpu.HBM)
+
+
+def in_smem(x):
+    return pltpu.with_memory_space_constraint(x, pltpu.SMEM)
 
 
 def divisor(n, most):
@@ -63,11 +73,7 @@
 
 def exchange(sends):
     routes = swaps()
-    order = (0, 1, 3, 2)
-    got = [None] * 4
-    for i in order:
-        got[i] = lax.ppermute(sends[i], ("region", "sub"), routes[i])
-    return got
+    return [lax.ppermute(x, ("region", "sub"), routes[k]) for x, k in zip(sends, ORDER)]
 
 
 class Layout:
@@ -84,6 +90,9 @@
         self.n_out = self.n_far + 1
         self.size = self.n_out + 1
 
+    def lists(self, refs):
+        return [(ref, self.starts[k], self.counts[k]) for ref, k in zip(refs, ORDER)]
+
 
 def pack(place, block, got):
     return place + block * 1024 + got * (1 << 20)
@@ -107,20 +116,39 @@
     return jnp.maximum(row, 0)
 
 
-def first_send_kernel(lay, sub_ref, reg_ref, probes_ref, *send_refs):
-    for n, (start, count) in enumerate(zip(lay.starts, lay.counts)):
+def first_send_kernel(lay, first, sub_hbm, reg_hbm, slot_hbm, coeff_hbm, probes_hbm, blocks_hbm,
+                      s0, s1, s2, s3, sub_ref, reg_ref, slot_ref, coeff_ref, ext_ref, raw_ref, probes, sems):
+    pairs = (
+        (sub_hbm, sub_ref),
+        (reg_hbm, reg_ref),
+        (probes_hbm, probes),
+        (slot_hbm, slot_ref),
+        (coeff_hbm, coeff_ref),
+        (blocks_hbm.at[pl.ds(0, first)], raw_ref),
+    )
+    loads = [pltpu.make_async_copy(a, b, sems.at[n]) for n, (a, b) in enumerate(pairs)]
+    for load in loads:
+        load.start()
+    loads[0].wait()
+    loads[1].wait()
+    at = [send_row(lay, sub_ref, reg_ref, j) * 128 for j in range(lay.halo)]
+    loads[2].wait()
+    for ref, start, count in lay.lists((s0, s1, s2, s3)):
         for j in range(count):
-            row = send_row(lay, sub_ref, reg_ref, start + j)
-            send_refs[n][j] = probes_ref[:, pl.ds(pl.multiple_of(row * 128, 128), 128)]
-
-
-def prologue_kernel(lay, chunk, slot_ref, sub_ref, reg_ref, coeff_ref, probes_ref, blocks_ref,
-                    bt_ref, x_ref, y_ref, t_ref, ext_ref, info_ref, raw, sems):
+            ref[j] = probes[:, pl.ds(pl.multiple_of(at[start + j], 128), 128)]
+    for i in range(lay.rows):
+        ext_ref[i] = probes[:, i * 128:(i + 1) * 128]
+    ext_ref[lay.rows] = jnp.zeros_like(ext_ref[lay.rows])
+    for load in loads[3:]:
+        load.wait()
+
+
+def prologue_kernel(lay, first, cuts, slot_ref, sub_ref, reg_ref, coeff_ref, ext_ref, raw0, blocks_hbm,
+                    bt_ref, x_ref, y_ref, t_ref, info_ref, raw, sems):
     rows = lay.rows
-    chunks = rows // chunk
     copies = [
-        pltpu.make_async_copy(blocks_ref.at[pl.ds(c * chunk, chunk)], raw.at[pl.ds(c * chunk, chunk)], sems.at[c])
-        for c in range(chunks)
+        pltpu.make_async_copy(blocks_hbm.at[pl.ds(a, b - a)], raw.at[pl.ds(a - first, b - a)], sems.at[n])
+        for n, (a, b) in enumerate(zip(cuts, cuts[1:]))
     ]
     for copy in copies:
         copy.start()
@@ -135,53 +163,52 @@
         return jnp.where(o < 2 * hs, sub_at, reg_at)
 
     c0 = coeff_ref[0]
-    for i in range(rows):
-        v = probes_ref[:, i * 128:(i + 1) * 128]
-        ext_ref[i] = v
-        x_ref[i] = v.astype(F32)
-        t_ref[i] = c0 * v.astype(F32)
-    ext_ref[rows] = jnp.zeros_like(ext_ref[rows])
     y_ref[rows] = jnp.zeros_like(y_ref[rows])
     x_ref[rows] = jnp.zeros_like(x_ref[rows])
-
-    def many(c, far):
-        pltpu.make_async_copy(blocks_ref.at[pl.ds(c * chunk, chunk)], raw.at[pl.ds(c * chunk, chunk)], sems.at[c]).wait()
-        for u in range(chunk):
-            i = c * chunk + u
+    t_ref[rows] = jnp.zeros_like(t_ref[rows])
+
+    def many(source, begin, end, far):
+        for i in range(begin, end):
             at = []
             for k in range(3):
-                slot = slot_ref[i, k]
+                slot = slot_ref[k, i]
                 at.append(jnp.where(slot < rows, slot, rows))
                 info_ref[lay.loc + 3 * i + k] = at[k]
                 if k > 0:
                     info_ref[lay.far + far] = pack(i, 3 * i + k, jnp.maximum(received(slot), 0))
                     far = far + jnp.where(slot < rows, 0, 1)
-            turned = [raw[i, k].T for k in range(3)]
+            turned = [source(i, k).T for k in range(3)]
             for k in range(3):
                 bt_ref[3 * i + k] = turned[k]
             x = jnp.concatenate([ext_ref[at[k]] for k in range(3)], 1)
             y_ref[i] = dot(x, jnp.concatenate(turned, 0))
+            v = ext_ref[i].astype(F32)
+            x_ref[i] = v
+            t_ref[i] = c0 * v
         return far
 
-    far = lax.fori_loop(0, chunks, many, jnp.int32(0))
-    for u in range(BATCH):
-        info_ref[lay.far + far + u] = pack(rows, 0, 0)
-    info_ref[lay.n_far] = far
+    far = many(lambda i, k: raw0[i, k], 0, first, jnp.int32(0))
     out = jnp.int32(0)
     for j in range(lay.halo):
         row = send_row(lay, sub_ref, reg_ref, j)
         info_ref[lay.tab + j] = row
         for k in (1, 2):
-            slot = slot_ref[row, k]
+            slot = slot_ref[k, row]
             info_ref[lay.out + out] = pack(j, 3 * row + k, jnp.maximum(received(slot), 0))
             out = out + jnp.where(slot < rows, 0, 1)
     for u in range(BATCH):
         info_ref[lay.out + out + u] = pack(lay.halo, 0, 0)
     info_ref[lay.n_out] = out
+    for copy, a, b in zip(copies, cuts, cuts[1:]):
+        copy.wait()
+        far = many(lambda i, k: raw[i - first, k], a, b, far)
+    for u in range(BATCH):
+        info_ref[lay.far + far + u] = pack(rows, 0, 0)
+    info_ref[lay.n_far] = far
 
 
 def gather_received(lay, got_refs, got):
-    for ref, start, count in zip(got_refs, lay.starts, lay.counts):
+    for ref, start, count in lay.lists(got_refs):
         for j in range(count):
             got[start + j] = ref[j]
 
@@ -205,7 +232,7 @@
     for j in range(lay.halo):
         held[j] = y_ref[info_ref[lay.tab + j]]
     add_received(factor, info_ref, lay.out, info_ref[lay.n_out], bt_ref, got, held)
-    for ref, start, count in zip((s0, s1, s2, s3), lay.starts, lay.counts):
+    for ref, start, count in lay.lists((s0, s1, s2, s3)):
         for j in range(count):
             ref[j] = held[start + j].astype(BF16)
 
@@ -250,39 +277,40 @@
     rows, _, width, _ = blocks.shape
     count = probes.shape[0]
     lay = Layout(rows, send_sub.shape[2], send_reg.shape[2])
-    chunk = divisor(rows, 13)
     unroll = divisor(rows, 52)
     small, large = 4 << 20, 20 << 20
 
     sends_shape = [pltpu.VMEM((n, count, width), BF16) for n in lay.counts]
+    sends_shape = [sends_shape[k] for k in ORDER]
     got_scratch = pltpu.VMEM((lay.halo, count, width), BF16)
     state = pltpu.VMEM((rows + 1, count, width), F32)
 
-    sends = pl.pallas_call(
-        functools.partial(first_send_kernel, lay),
-        in_specs=[SMEM, SMEM, VMEM],
-        out_specs=[VMEM] * 4,
-        out_shape=sends_shape,
+    slots = col_slot.T
+    first = min(FIRST, rows // 2)
+    cuts = sorted(set(list(range(first, rows, 26)) + [max(first, rows - 13), rows]))
+    smalls = (send_sub, send_reg, slots, coeffs)
+    ext_shape = pltpu.VMEM((rows + 1, count, width), BF16)
+    results = pl.pallas_call(
+        functools.partial(first_send_kernel, lay, first),
+        in_specs=[HBM] * 6,
+        out_specs=[VMEM] * 4 + [SMEM] * 4 + [VMEM] * 2,
+        out_shape=sends_shape + [pltpu.SMEM(a.shape, a.dtype) for a in smalls]
+        + [ext_shape, pltpu.VMEM((first, 3, width, width), BF16)],
+        scratch_shapes=[pltpu.VMEM(probes.shape, BF16), pltpu.SemaphoreType.DMA((6,))],
         compiler_params=pltpu.CompilerParams(vmem_limit_bytes=small),
         name="first_send",
-    )(send_sub, send_reg, probes)
+    )(*[in_hbm(a) for a in smalls + (probes, blocks)])
+    sends, (subs, regs, slots, coeffs, ext, raw0) = results[:4], results[4:]
     got = exchange(sends)
-    bt, x, y, t, ext, info = pl.pallas_call(
-        functools.partial(prologue_kernel, lay, chunk),
-        in_specs=[SMEM, SMEM, SMEM, SMEM, VMEM, HBM],
-        out_specs=[VMEM] * 5 + [SMEM],
-        out_shape=[
-            pltpu.VMEM((3 * rows, width, width), BF16),
-            state,
-            state,
-            pltpu.VMEM((rows + 1, count, width), F32),
-            pltpu.VMEM((rows + 1, count, width), BF16),
-            jax.ShapeDtypeStruct((lay.size,), I32),
-        ],
-        scratch_shapes=[pltpu.VMEM((rows, 3, width, width), BF16), pltpu.SemaphoreType.DMA((rows // chunk,))],
+    bt, x, y, t, info = pl.pallas_call(
+        functools.partial(prologue_kernel, lay, first, cuts),
+        in_specs=[SMEM] * 4 + [VMEM] * 2 + [HBM],
+        out_specs=[VMEM] * 4 + [SMEM],
+        out_shape=[pltpu.VMEM((3 * rows, width, width), BF16), state, state, state, pltpu.SMEM((lay.size,), I32)],
+        scratch_shapes=[pltpu.VMEM((rows - first, 3, width, width), BF16), pltpu.SemaphoreType.DMA((len(cuts) - 1,))],
         compiler_params=pltpu.CompilerParams(vmem_limit_bytes=large),
         name="prologue",
-    )(col_slot, send_sub, send_reg, coeffs, probes, pltpu.with_memory_space_constraint(blocks, pltpu.HBM))
+    )(*[in_smem(a) for a in (slots, subs, regs, coeffs)], in_vmem(ext), in_vmem(raw0), in_hbm(blocks))
     for step in range(1, DEG):
         y, *sends = pl.pallas_call(
             functools.partial(send_kernel, lay, 1.0 if step == 1 else 2.0),
@@ -293,7 +321,7 @@
             input_output_aliases={2: 0},
             compiler_params=pltpu.CompilerParams(vmem_limit_bytes=small),
             name="send",
-        )(info, in_vmem(bt), in_vmem(y), *[in_vmem(g) for g in got])
+        )(in_smem(info), in_vmem(bt), in_vmem(y), *[in_vmem(g) for g in got])
         later = exchange(sends)
         x, y, t, ext = pl.pallas_call(
             functools.partial(step_kernel, lay, step, unroll),
@@ -305,7 +333,7 @@
             compiler_params=pltpu.CompilerParams(vmem_limit_bytes=small),
             cost_estimate=pl.CostEstimate(flops=2 * rows * 3 * width * width * count, bytes_accessed=1 << 20, transcendentals=0),
             name="step",
-        )(info, coeffs, in_vmem(bt), *[in_vmem(g) for g in got], in_vmem(x), in_vmem(y), in_vmem(t), in_vmem(ext))
+        )(in_smem(info), in_smem(coeffs), in_vmem(bt), *[in_vmem(g) for g in got], in_vmem(x), in_vmem(y), in_vmem(t), in_vmem(ext))
         x, y = y, x
         got = later
     out, _ = pl.pallas_call(
@@ -317,7 +345,7 @@
         input_output_aliases={3: 1},
         compiler_params=pltpu.CompilerParams(vmem_limit_bytes=small),
         name="final",
-    )(info, coeffs, in_vmem(bt), in_vmem(t), *[in_vmem(g) for g in got])
+    )(in_smem(info), in_smem(coeffs), in_vmem(bt), in_vmem(t), *[in_vmem(g) for g in got])
     return out
 
 

time: 77.1 us -> 61.3 us (0.80)
  Pallas kernels: 38.6 us -> 28.2 us
  local copies, waits for them, and re-layouts: 6.46 us -> 0 us
  waiting for transfers between devices: 0.08 us -> 2.16 us
    unnamed x17 -> x0, local copies, waits for them, and re-layouts: 6.46 us -> none
    pallas_call x7, Pallas kernels: 21.8 us -> 16.9 us  [local(): pl.pallas_call(functools.partial(step_kernel, lay, step, unroll), in_spec...]
    pallas_call x7, Pallas kernels: 5.85 us -> 2.33 us  [local(): pl.pallas_call(functools.partial(send_kernel, lay, 1.0 if step == 1 else...]
    ppermute x32, waiting for transfers between devices: 0.08 us -> 2.16 us  [exchange(): lax.ppermute(x, ('region', 'sub'), routes[k])]
    pallas_call x2, Pallas kernels: 8.61 us -> 7.39 us  [the longest x1 5.77 us: local(): pl.pallas_call(functools.partial(prologue_kernel, lay, first, cuts), in_s...]
  transfers between devices with their start and end apart: 32 -> 32, of which waited for: 0 -> 5; matrix products, arithmetic and copies ran while one was open for 1% -> 0% of each run, Pallas kernels for 39% -> 37%
where the time goes in v1:
time: 61.3 us; the launch traced here: 61.1 us
  starting transfers between devices  30.5 us (50%)
  Pallas kernels  28.2 us (46%)
  waiting for transfers between devices  2.16 us (4%)
    ppermute x32, starting transfers between devices, exchange(): lax.ppermute(x, ('region', 'sub'), routes[k])  30.5 us
    pallas_call x7, Pallas kernels, local(): pl.pallas_call(functools.partial(step_kernel, lay, step, unroll), in_spec...  16.9 us
    pallas_call x1, Pallas kernels, local(): pl.pallas_call(functools.partial(prologue_kernel, lay, first, cuts), in_s...  5.77 us
    pallas_call x7, Pallas kernels, local(): pl.pallas_call(functools.partial(send_kernel, lay, 1.0 if step == 1 else...  2.33 us
    ppermute x32, waiting for transfers between devices, exchange(): lax.ppermute(x, ('region', 'sub'), routes[k])  2.16 us
    pallas_call x1, Pallas kernels, local(): pl.pallas_call(functools.partial(first_send_kernel, lay, first), in_specs...  1.62 us
    pallas_call x1, Pallas kernels, local(): pl.pallas_call(functools.partial(final_kernel, lay), in_specs=[SMEM, SMEM...  1.58 us
  transfers between devices with their start and end apart: 32, of which 5 were waited for; matrix products, arithmetic and copies ran while one was open for 0% of the time, Pallas kernels for 37%

profile of v1, /device:TPU:1, one launch (start us, length us, event | category | flops | bytes accessed | tf_op | source)
XLA Modules:
  0.0 61.1 jit_solution(5723584974814343103)
XLA Ops:
  0.0 1.6 %first_send.1 = (bf16[8,32,128]{2,1,0:T(8,128)(2,1)S(1)}, bf16[8,32,128]{2,1,0:T(8,128)(2,1)S(1)}, bf16[4,32,128]{2,1,0:T(8,128)(2,1)S(1)}, bf16[4,32,128]{2,1,0...) custom-call(s32[1,2,8]{2,1,0:T(2,128)} %sub_hbm.1, ...), custom_call_target="tpu_custom_call" | custom-call | tf_op jit(solution)/shard_map/first_send/pallas_call | solution.py:293
  1.6 2.1 %collective-permute-start = (bf16[8,32,128]{2,1,0:T(8,128)(2,1)S(1)}, bf16[8,32,128]{2,1,0:T(8,128)(2,1)S(1)}, u32[]{:S(2)}, u32[]{:S(2)}) collective-permute-start(bf16[8,32,128]{2,1,0:T(8,128)(2,1)S(1)} %get-tuple-element.89), channel_id=1, source_target_pairs={{0,1},{1,0},{2,3},{3,2},{4,5},{5,4},{6,7},{7,6},{8,9},{9,8},{10,11... | collective-permute-start | bytes 196616 | tf_op jit(solution)/shard_map/ppermute | solution.py:76
  3.7 1.0 %collective-permute-start.1 = (bf16[8,32,128]{2,1,0:T(8,128)(2,1)S(1)}, bf16[8,32,128]{2,1,0:T(8,128)(2,1)S(1)}, u32[]{:S(2)}, u32[]{:S(2)}) collective-permute-start(bf16[8,32,128]{2,1,0:T(8,128)(2,1)S(1)} %get-tuple-element.90), channel_id=1, source_target_pairs={{0,8},{1,2},{2,1},{3,4},{4,3},{5,6},{6,5},{7,15},{8,0},{9,10},{10,... | collective-permute-start | bytes 196616 | tf_op jit(solution)/shard_map/ppermute | solution.py:76
  4.7 1.1 %collective-permute-start.2 = (bf16[4,32,128]{2,1,0:T(8,128)(2,1)S(1)}, bf16[4,32,128]{2,1,0:T(8,128)(2,1)S(1)}, u32[]{:S(2)}, u32[]{:S(2)}) collective-permute-start(bf16[4,32,128]{2,1,0:T(8,128)(2,1)S(1)} %get-tuple-element.91), channel_id=1, source_target_pairs={{0,24},{1,25},{2,26},{3,27},{4,28},{5,29},{6,30},{7,31},{8,16},{9,... | collective-permute-start | bytes 98312 | tf_op jit(solution)/shard_map/ppermute | solution.py:76
  6.3 5.8 %prologue.1 = (bf16[312,128,128]{2,1,0:T(8,128)(2,1)S(1)}, f32[105,32,128]{2,1,0:T(8,128)S(1)}, f32[105,32,128]{2,1,0:T(8,128)S(1)}, f32[105,32,128]{2,1,0:T(8,128)S(1)}, s32[626]{0:T(1024)S(4)}) custom-call(s32[3,104]{1,0:T(4,128)S(4)} %get-tuple-element.81.slot_ref, s32[1,2,8]{2,1,0:T(2,128)S(4)} %get-tuple-element.82.sub_ref, ...), custom_call_target="tpu_custom_call" | custom-call | tf_op jit(solution)/shard_map/prologue/pallas_call | solution.py:305
  12.5 2.3 %collective-permute-start.4 = (bf16[8,32,128]{2,1,0:T(8,128)(2,1)S(1)}, bf16[8,32,128]{2,1,0:T(8,128)(2,1)S(1)}, u32[]{:S(2)}, u32[]{:S(2)}) collective-permute-start(bf16[8,32,128]{2,1,0:T(8,128)(2,1)S(1)} %get-tuple-element.98), channel_id=1, source_target_pairs={{0,1},{1,0},{2,3},{3,2},{4,5},{5,4},{6,7},{7,6},{8,9},{9,8},{10,11... | collective-permute-start | bytes 196616 | tf_op jit(solution)/shard_map/ppermute | solution.py:76
  15.9 2.4 %step.7 = (f32[105,32,128]{2,1,0:T(8,128)S(1)}, f32[105,32,128]{2,1,0:T(8,128)S(1)}, f32[105,32,128]{2,1,0:T(8,128)S(1)}, bf16[105,32,128]{2,1,0:T(8,128)(2,1)S(1)}) custom-call(s32[626]{0:T(1024)S(4)} %get-tuple-element.87.info_ref, f32[9]{0:T(128)S(4)} %get-tuple-element.84.coeff_ref, ...), custom_call_target="tpu_custom_call", output_to_operand_aliasing={{0}: (7, {}), {1}: (8, {}), {2}: (9, {}), {3}: (10, {})} | custom-call | flops 327155712 | bytes 1048576 | tf_op jit(solution)/shard_map/step/pallas_call | solution.py:326
  19.3 2.3 %collective-permute-start.8 = (bf16[8,32,128]{2,1,0:T(8,128)(2,1)S(1)}, bf16[8,32,128]{2,1,0:T(8,128)(2,1)S(1)}, u32[]{:S(2)}, u32[]{:S(2)}) collective-permute-start(bf16[8,32,128]{2,1,0:T(8,128)(2,1)S(1)} %get-tuple-element.102), channel_id=1, source_target_pairs={{0,1},{1,0},{2,3},{3,2},{4,5},{5,4},{6,7},{7,6},{8,9},{9,8},{10,11... | collective-permute-start | bytes 196616 | tf_op jit(solution)/shard_map/ppermute | solution.py:76
  21.6 0.8 %collective-permute-start.9 = (bf16[8,32,128]{2,1,0:T(8,128)(2,1)S(1)}, bf16[8,32,128]{2,1,0:T(8,128)(2,1)S(1)}, u32[]{:S(2)}, u32[]{:S(2)}) collective-permute-start(bf16[8,32,128]{2,1,0:T(8,128)(2,1)S(1)} %get-tuple-element.103), channel_id=1, source_target_pairs={{0,8},{1,2},{2,1},{3,4},{4,3},{5,6},{6,5},{7,15},{8,0},{9,10},{10,... | collective-permute-start | bytes 196616 | tf_op jit(solution)/shard_map/ppermute | solution.py:76
  23.5 2.4 %step.8 = (f32[105,32,128]{2,1,0:T(8,128)S(1)}, f32[105,32,128]{2,1,0:T(8,128)S(1)}, f32[105,32,128]{2,1,0:T(8,128)S(1)}, bf16[105,32,128]{2,1,0:T(8,128)(2,1)S(1)}) custom-call(s32[626]{0:T(1024)S(4)} %get-tuple-element.87.info_ref, f32[9]{0:T(128)S(4)} %get-tuple-element.84.coeff_ref, ...), custom_call_target="tpu_custom_call", output_to_operand_aliasing={{0}: (7, {}), {1}: (8, {}), {2}: (9, {}), {3}: (10, {})} | custom-call | flops 327155712 | bytes 1048576 | tf_op jit(solution)/shard_map/step/pallas_call | solution.py:326
  26.2 2.8 %collective-permute-start.12 = (bf16[8,32,128]{2,1,0:T(8,128)(2,1)S(1)}, bf16[8,32,128]{2,1,0:T(8,128)(2,1)S(1)}, u32[]{:S(2)}, u32[]{:S(2)}) collective-permute-start(bf16[8,32,128]{2,1,0:T(8,128)(2,1)S(1)} %get-tuple-element.116), channel_id=1, source_target_pairs={{0,1},{1,0},{2,3},{3,2},{4,5},{5,4},{6,7},{7,6},{8,9},{9,8},{10,11... | collective-permute-start | bytes 196616 | tf_op jit(solution)/shard_map/ppermute | solution.py:76
  30.2 2.4 %step.9 = (f32[105,32,128]{2,1,0:T(8,128)S(1)}, f32[105,32,128]{2,1,0:T(8,128)S(1)}, f32[105,32,128]{2,1,0:T(8,128)S(1)}, bf16[105,32,128]{2,1,0:T(8,128)(2,1)S(1)}) custom-call(s32[626]{0:T(1024)S(4)} %get-tuple-element.87.info_ref, f32[9]{0:T(128)S(4)} %get-tuple-element.84.coeff_ref, ...), custom_call_target="tpu_custom_call", output_to_operand_aliasing={{0}: (7, {}), {1}: (8, {}), {2}: (9, {}), {3}: (10, {})} | custom-call | flops 327155712 | bytes 1048576 | tf_op jit(solution)/shard_map/step/pallas_call | solution.py:326
  33.5 1.3 %collective-permute-start.16 = (bf16[8,32,128]{2,1,0:T(8,128)(2,1)S(1)}, bf16[8,32,128]{2,1,0:T(8,128)(2,1)S(1)}, u32[]{:S(2)}, u32[]{:S(2)}) collective-permute-start(bf16[8,32,128]{2,1,0:T(8,128)(2,1)S(1)} %get-tuple-element.120), channel_id=1, source_target_pairs={{0,1},{1,0},{2,3},{3,2},{4,5},{5,4},{6,7},{7,6},{8,9},{9,8},{10,11... | collective-permute-start | bytes 196616 | tf_op jit(solution)/shard_map/ppermute | solution.py:76
  34.9 1.0 %collective-permute-start.17 = (bf16[8,32,128]{2,1,0:T(8,128)(2,1)S(1)}, bf16[8,32,128]{2,1,0:T(8,128)(2,1)S(1)}, u32[]{:S(2)}, u32[]{:S(2)}) collective-permute-start(bf16[8,32,128]{2,1,0:T(8,128)(2,1)S(1)} %get-tuple-element.121), channel_id=1, source_target_pairs={{0,8},{1,2},{2,1},{3,4},{4,3},{5,6},{6,5},{7,15},{8,0},{9,10},{10,... | collective-permute-start | bytes 196616 | tf_op jit(solution)/shard_map/ppermute | solution.py:76
  36.6 2.6 %step.10 = (f32[105,32,128]{2,1,0:T(8,128)S(1)}, f32[105,32,128]{2,1,0:T(8,128)S(1)}, f32[105,32,128]{2,1,0:T(8,128)S(1)}, bf16[105,32,128]{2,1,0:T(8,128)(2,1)S(1)}) custom-call(s32[626]{0:T(1024)S(4)} %get-tuple-element.87.info_ref, f32[9]{0:T(128)S(4)} %get-tuple-element.84.coeff_ref, ...), custom_call_target="tpu_custom_call", output_to_operand_aliasing={{0}: (7, {}), {1}: (8, {}), {2}: (9, {}), {3}: (10, {})} | custom-call | flops 327155712 | bytes 1048576 | tf_op jit(solution)/shard_map/step/pallas_call | solution.py:326
  39.6 2.8 %collective-permute-start.20 = (bf16[8,32,128]{2,1,0:T(8,128)(2,1)S(1)}, bf16[8,32,128]{2,1,0:T(8,128)(2,1)S(1)}, u32[]{:S(2)}, u32[]{:S(2)}) collective-permute-start(bf16[8,32,128]{2,1,0:T(8,128)(2,1)S(1)} %get-tuple-element.134), channel_id=1, source_target_pairs={{0,1},{1,0},{2,3},{3,2},{4,5},{5,4},{6,7},{7,6},{8,9},{9,8},{10,11... | collective-permute-start | bytes 196616 | tf_op jit(solution)/shard_map/ppermute | solution.py:76
  42.4 0.8 %collective-permute-start.21 = (bf16[8,32,128]{2,1,0:T(8,128)(2,1)S(1)}, bf16[8,32,128]{2,1,0:T(8,128)(2,1)S(1)}, u32[]{:S(2)}, u32[]{:S(2)}) collective-permute-start(bf16[8,32,128]{2,1,0:T(8,128)(2,1)S(1)} %get-tuple-element.135), channel_id=1, source_target_pairs={{0,8},{1,2},{2,1},{3,4},{4,3},{5,6},{6,5},{7,15},{8,0},{9,10},{10,... | collective-permute-start | bytes 196616 | tf_op jit(solution)/shard_map/ppermute | solution.py:76
  43.5 2.4 %step.11 = (f32[105,32,128]{2,1,0:T(8,128)S(1)}, f32[105,32,128]{2,1,0:T(8,128)S(1)}, f32[105,32,128]{2,1,0:T(8,128)S(1)}, bf16[105,32,128]{2,1,0:T(8,128)(2,1)S(1)}) custom-call(s32[626]{0:T(1024)S(4)} %get-tuple-element.87.info_ref, f32[9]{0:T(128)S(4)} %get-tuple-element.84.coeff_ref, ...), custom_call_target="tpu_custom_call", output_to_operand_aliasing={{0}: (7, {}), {1}: (8, {}), {2}: (9, {}), {3}: (10, {})} | custom-call | flops 327155712 | bytes 1048576 | tf_op jit(solution)/shard_map/step/pallas_call | solution.py:326
  46.9 1.3 %collective-permute-start.24 = (bf16[8,32,128]{2,1,0:T(8,128)(2,1)S(1)}, bf16[8,32,128]{2,1,0:T(8,128)(2,1)S(1)}, u32[]{:S(2)}, u32[]{:S(2)}) collective-permute-start(bf16[8,32,128]{2,1,0:T(8,128)(2,1)S(1)} %get-tuple-element.138), channel_id=1, source_target_pairs={{0,1},{1,0},{2,3},{3,2},{4,5},{5,4},{6,7},{7,6},{8,9},{9,8},{10,11... | collective-permute-start | bytes 196616 | tf_op jit(solution)/shard_map/ppermute | solution.py:76
  48.2 1.1 %collective-permute-start.25 = (bf16[8,32,128]{2,1,0:T(8,128)(2,1)S(1)}, bf16[8,32,128]{2,1,0:T(8,128)(2,1)S(1)}, u32[]{:S(2)}, u32[]{:S(2)}) collective-permute-start(bf16[8,32,128]{2,1,0:T(8,128)(2,1)S(1)} %get-tuple-element.139), channel_id=1, source_target_pairs={{0,8},{1,2},{2,1},{3,4},{4,3},{5,6},{6,5},{7,15},{8,0},{9,10},{10,... | collective-permute-start | bytes 196616 | tf_op jit(solution)/shard_map/ppermute | solution.py:76
  50.2 2.4 %step.12 = (f32[105,32,128]{2,1,0:T(8,128)S(1)}, f32[105,32,128]{2,1,0:T(8,128)S(1)}, f32[105,32,128]{2,1,0:T(8,128)S(1)}, bf16[105,32,128]{2,1,0:T(8,128)(2,1)S(1)}) custom-call(s32[626]{0:T(1024)S(4)} %get-tuple-element.87.info_ref, f32[9]{0:T(128)S(4)} %get-tuple-element.84.coeff_ref, ...), custom_call_target="tpu_custom_call", output_to_operand_aliasing={{0}: (7, {}), {1}: (8, {}), {2}: (9, {}), {3}: (10, {})} | custom-call | flops 327155712 | bytes 1048576 | tf_op jit(solution)/shard_map/step/pallas_call | solution.py:326
  53.0 2.4 %collective-permute-start.28 = (bf16[8,32,128]{2,1,0:T(8,128)(2,1)S(1)}, bf16[8,32,128]{2,1,0:T(8,128)(2,1)S(1)}, u32[]{:S(2)}, u32[]{:S(2)}) collective-permute-start(bf16[8,32,128]{2,1,0:T(8,128)(2,1)S(1)} %get-tuple-element.152), channel_id=1, source_target_pairs={{0,1},{1,0},{2,3},{3,2},{4,5},{5,4},{6,7},{7,6},{8,9},{9,8},{10,11... | collective-permute-start | bytes 196616 | tf_op jit(solution)/shard_map/ppermute | solution.py:76
  56.8 2.4 %step.13 = (f32[105,32,128]{2,1,0:T(8,128)S(1)}, f32[105,32,128]{2,1,0:T(8,128)S(1)}, f32[105,32,128]{2,1,0:T(8,128)S(1)}, bf16[105,32,128]{2,1,0:T(8,128)(2,1)S(1)}) custom-call(s32[626]{0:T(1024)S(4)} %get-tuple-element.87.info_ref, f32[9]{0:T(128)S(4)} %get-tuple-element.84.coeff_ref, ...), custom_call_target="tpu_custom_call", output_to_operand_aliasing={{0}: (7, {}), {1}: (8, {}), {2}: (9, {}), {3}: (10, {})} | custom-call | flops 327155712 | bytes 1048576 | tf_op jit(solution)/shard_map/step/pallas_call | solution.py:326
  59.5 1.6 %final.1 = (f32[32,13312]{1,0:T(8,128)}, f32[105,32,128]{2,1,0:T(8,128)S(1)}) custom-call(s32[626]{0:T(1024)S(4)} %get-tuple-element.87.info_ref, f32[9]{0:T(128)S(4)} %get-tuple-element.84.coeff_ref, bf16[312,128,128]{2,1,0:T(8,128)(2,1)S(1)} %get-tuple-element.88.bt_ref, ...), custom_call_target="tpu_custom_call", output_to_operand_aliasing={{1}: (3, {})} | custom-call | tf_op jit(solution)/shard_map/final/pallas_call | solution.py:339
  (57 shorter events, 11.8 us)
Async XLA Ops:
  1.6 10.5 %collective-permute-start = (bf16[8,32,128]{2,1,0:T(8,128)(2,1)S(1)}, bf16[8,32,128]{2,1,0:T(8,128)(2,1)S(1)}, u32[]{:S(2)}, u32[]{:S(2)}) collective-permute-start(bf16[8,32,128]{2,1,0:T(8,128)(2,1)S(1)} %get-tuple-element.89), channel_id=1, source_target_pairs={{0,1},{1,0},{2,3},{3,2},{4,5},{5,4},{6,7},{7,6},{8,9},{9,8},{10,11... | collective-permute-start | bytes 196616 | tf_op jit(solution)/shard_map/ppermute | solution.py:76
  3.7 8.4 %collective-permute-start.1 = (bf16[8,32,128]{2,1,0:T(8,128)(2,1)S(1)}, bf16[8,32,128]{2,1,0:T(8,128)(2,1)S(1)}, u32[]{:S(2)}, u32[]{:S(2)}) collective-permute-start(bf16[8,32,128]{2,1,0:T(8,128)(2,1)S(1)} %get-tuple-element.90), channel_id=1, source_target_pairs={{0,8},{1,2},{2,1},{3,4},{4,3},{5,6},{6,5},{7,15},{8,0},{9,10},{10,... | collective-permute-start | bytes 196616 | tf_op jit(solution)/shard_map/ppermute | solution.py:76
  4.7 7.4 %collective-permute-start.2 = (bf16[4,32,128]{2,1,0:T(8,128)(2,1)S(1)}, bf16[4,32,128]{2,1,0:T(8,128)(2,1)S(1)}, u32[]{:S(2)}, u32[]{:S(2)}) collective-permute-start(bf16[4,32,128]{2,1,0:T(8,128)(2,1)S(1)} %get-tuple-element.91), channel_id=1, source_target_pairs={{0,24},{1,25},{2,26},{3,27},{4,28},{5,29},{6,30},{7,31},{8,16},{9,... | collective-permute-start | bytes 98312 | tf_op jit(solution)/shard_map/ppermute | solution.py:76
  5.8 6.3 %collective-permute-start.3 = (bf16[4,32,128]{2,1,0:T(8,128)(2,1)S(1)}, bf16[4,32,128]{2,1,0:T(8,128)(2,1)S(1)}, u32[]{:S(2)}, u32[]{:S(2)}) collective-permute-start(bf16[4,32,128]{2,1,0:T(8,128)(2,1)S(1)} %get-tuple-element.92), channel_id=1, source_target_pairs={{0,8},{1,9},{2,10},{3,11},{4,12},{5,13},{6,14},{7,15},{8,0},{9,1},... | collective-permute-start | bytes 98312 | tf_op jit(solution)/shard_map/ppermute | solution.py:76
  12.5 6.4 %collective-permute-start.4 = (bf16[8,32,128]{2,1,0:T(8,128)(2,1)S(1)}, bf16[8,32,128]{2,1,0:T(8,128)(2,1)S(1)}, u32[]{:S(2)}, u32[]{:S(2)}) collective-permute-start(bf16[8,32,128]{2,1,0:T(8,128)(2,1)S(1)} %get-tuple-element.98), channel_id=1, source_target_pairs={{0,1},{1,0},{2,3},{3,2},{4,5},{5,4},{6,7},{7,6},{8,9},{9,8},{10,11... | collective-permute-start | bytes 196616 | tf_op jit(solution)/shard_map/ppermute | solution.py:76
  14.8 4.1 %collective-permute-start.5 = (bf16[8,32,128]{2,1,0:T(8,128)(2,1)S(1)}, bf16[8,32,128]{2,1,0:T(8,128)(2,1)S(1)}, u32[]{:S(2)}, u32[]{:S(2)}) collective-permute-start(bf16[8,32,128]{2,1,0:T(8,128)(2,1)S(1)} %get-tuple-element.99), channel_id=1, source_target_pairs={{0,8},{1,2},{2,1},{3,4},{4,3},{5,6},{6,5},{7,15},{8,0},{9,10},{10,... | collective-permute-start | bytes 196616 | tf_op jit(solution)/shard_map/ppermute | solution.py:76
  15.6 3.3 %collective-permute-start.6 = (bf16[4,32,128]{2,1,0:T(8,128)(2,1)S(1)}, bf16[4,32,128]{2,1,0:T(8,128)(2,1)S(1)}, u32[]{:S(2)}, u32[]{:S(2)}) collective-permute-start(bf16[4,32,128]{2,1,0:T(8,128)(2,1)S(1)} %get-tuple-element.100), channel_id=1, source_target_pairs={{0,24},{1,25},{2,26},{3,27},{4,28},{5,29},{6,30},{7,31},{8,16},{9,... | collective-permute-start | bytes 98312 | tf_op jit(solution)/shard_map/ppermute | solution.py:76
  15.6 3.3 %collective-permute-start.7 = (bf16[4,32,128]{2,1,0:T(8,128)(2,1)S(1)}, bf16[4,32,128]{2,1,0:T(8,128)(2,1)S(1)}, u32[]{:S(2)}, u32[]{:S(2)}) collective-permute-start(bf16[4,32,128]{2,1,0:T(8,128)(2,1)S(1)} %get-tuple-element.101), channel_id=1, source_target_pairs={{0,8},{1,9},{2,10},{3,11},{4,12},{5,13},{6,14},{7,15},{8,0},{9,1},... | collective-permute-start | bytes 98312 | tf_op jit(solution)/shard_map/ppermute | solution.py:76
  19.3 6.6 %collective-permute-start.8 = (bf16[8,32,128]{2,1,0:T(8,128)(2,1)S(1)}, bf16[8,32,128]{2,1,0:T(8,128)(2,1)S(1)}, u32[]{:S(2)}, u32[]{:S(2)}) collective-permute-start(bf16[8,32,128]{2,1,0:T(8,128)(2,1)S(1)} %get-tuple-element.102), channel_id=1, source_target_pairs={{0,1},{1,0},{2,3},{3,2},{4,5},{5,4},{6,7},{7,6},{8,9},{9,8},{10,11... | collective-permute-start | bytes 196616 | tf_op jit(solution)/shard_map/ppermute | solution.py:76
  21.6 4.3 %collective-permute-start.9 = (bf16[8,32,128]{2,1,0:T(8,128)(2,1)S(1)}, bf16[8,32,128]{2,1,0:T(8,128)(2,1)S(1)}, u32[]{:S(2)}, u32[]{:S(2)}) collective-permute-start(bf16[8,32,128]{2,1,0:T(8,128)(2,1)S(1)} %get-tuple-element.103), channel_id=1, source_target_pairs={{0,8},{1,2},{2,1},{3,4},{4,3},{5,6},{6,5},{7,15},{8,0},{9,10},{10,... | collective-permute-start | bytes 196616 | tf_op jit(solution)/shard_map/ppermute | solution.py:76
  22.4 3.5 %collective-permute-start.10 = (bf16[4,32,128]{2,1,0:T(8,128)(2,1)S(1)}, bf16[4,32,128]{2,1,0:T(8,128)(2,1)S(1)}, u32[]{:S(2)}, u32[]{:S(2)}) collective-permute-start(bf16[4,32,128]{2,1,0:T(8,128)(2,1)S(1)} %get-tuple-element.104), channel_id=1, source_target_pairs={{0,24},{1,25},{2,26},{3,27},{4,28},{5,29},{6,30},{7,31},{8,16},{9,... | collective-permute-start | bytes 98312 | tf_op jit(solution)/shard_map/ppermute | solution.py:76
  26.2 7.0 %collective-permute-start.12 = (bf16[8,32,128]{2,1,0:T(8,128)(2,1)S(1)}, bf16[8,32,128]{2,1,0:T(8,128)(2,1)S(1)}, u32[]{:S(2)}, u32[]{:S(2)}) collective-permute-start(bf16[8,32,128]{2,1,0:T(8,128)(2,1)S(1)} %get-tuple-element.116), channel_id=1, source_target_pairs={{0,1},{1,0},{2,3},{3,2},{4,5},{5,4},{6,7},{7,6},{8,9},{9,8},{10,11... | collective-permute-start | bytes 196616 | tf_op jit(solution)/shard_map/ppermute | solution.py:76
  29.1 4.1 %collective-permute-start.13 = (bf16[8,32,128]{2,1,0:T(8,128)(2,1)S(1)}, bf16[8,32,128]{2,1,0:T(8,128)(2,1)S(1)}, u32[]{:S(2)}, u32[]{:S(2)}) collective-permute-start(bf16[8,32,128]{2,1,0:T(8,128)(2,1)S(1)} %get-tuple-element.117), channel_id=1, source_target_pairs={{0,8},{1,2},{2,1},{3,4},{4,3},{5,6},{6,5},{7,15},{8,0},{9,10},{10,... | collective-permute-start | bytes 196616 | tf_op jit(solution)/shard_map/ppermute | solution.py:76
  29.9 3.3 %collective-permute-start.14 = (bf16[4,32,128]{2,1,0:T(8,128)(2,1)S(1)}, bf16[4,32,128]{2,1,0:T(8,128)(2,1)S(1)}, u32[]{:S(2)}, u32[]{:S(2)}) collective-permute-start(bf16[4,32,128]{2,1,0:T(8,128)(2,1)S(1)} %get-tuple-element.118), channel_id=1, source_target_pairs={{0,24},{1,25},{2,26},{3,27},{4,28},{5,29},{6,30},{7,31},{8,16},{9,... | collective-permute-start | bytes 98312 | tf_op jit(solution)/shard_map/ppermute | solution.py:76
  29.9 3.3 %collective-permute-start.15 = (bf16[4,32,128]{2,1,0:T(8,128)(2,1)S(1)}, bf16[4,32,128]{2,1,0:T(8,128)(2,1)S(1)}, u32[]{:S(2)}, u32[]{:S(2)}) collective-permute-start(bf16[4,32,128]{2,1,0:T(8,128)(2,1)S(1)} %get-tuple-element.119), channel_id=1, source_target_pairs={{0,8},{1,9},{2,10},{3,11},{4,12},{5,13},{6,14},{7,15},{8,0},{9,1},... | collective-permute-start | bytes 98312 | tf_op jit(solution)/shard_map/ppermute | solution.py:76
  33.5 5.7 %collective-permute-start.16 = (bf16[8,32,128]{2,1,0:T(8,128)(2,1)S(1)}, bf16[8,32,128]{2,1,0:T(8,128)(2,1)S(1)}, u32[]{:S(2)}, u32[]{:S(2)}) collective-permute-start(bf16[8,32,128]{2,1,0:T(8,128)(2,1)S(1)} %get-tuple-element.120), channel_id=1, source_target_pairs={{0,1},{1,0},{2,3},{3,2},{4,5},{5,4},{6,7},{7,6},{8,9},{9,8},{10,11... | collective-permute-start | bytes 196616 | tf_op jit(solution)/shard_map/ppermute | solution.py:76
  34.9 4.4 %collective-permute-start.17 = (bf16[8,32,128]{2,1,0:T(8,128)(2,1)S(1)}, bf16[8,32,128]{2,1,0:T(8,128)(2,1)S(1)}, u32[]{:S(2)}, u32[]{:S(2)}) collective-permute-start(bf16[8,32,128]{2,1,0:T(8,128)(2,1)S(1)} %get-tuple-element.121), channel_id=1, source_target_pairs={{0,8},{1,2},{2,1},{3,4},{4,3},{5,6},{6,5},{7,15},{8,0},{9,10},{10,... | collective-permute-start | bytes 196616 | tf_op jit(solution)/shard_map/ppermute | solution.py:76
  39.6 6.9 %collective-permute-start.20 = (bf16[8,32,128]{2,1,0:T(8,128)(2,1)S(1)}, bf16[8,32,128]{2,1,0:T(8,128)(2,1)S(1)}, u32[]{:S(2)}, u32[]{:S(2)}) collective-permute-start(bf16[8,32,128]{2,1,0:T(8,128)(2,1)S(1)} %get-tuple-element.134), channel_id=1, source_target_pairs={{0,1},{1,0},{2,3},{3,2},{4,5},{5,4},{6,7},{7,6},{8,9},{9,8},{10,11... | collective-permute-start | bytes 196616 | tf_op jit(solution)/shard_map/ppermute | solution.py:76
  42.4 4.1 %collective-permute-start.21 = (bf16[8,32,128]{2,1,0:T(8,128)(2,1)S(1)}, bf16[8,32,128]{2,1,0:T(8,128)(2,1)S(1)}, u32[]{:S(2)}, u32[]{:S(2)}) collective-permute-start(bf16[8,32,128]{2,1,0:T(8,128)(2,1)S(1)} %get-tuple-element.135), channel_id=1, source_target_pairs={{0,8},{1,2},{2,1},{3,4},{4,3},{5,6},{6,5},{7,15},{8,0},{9,10},{10,... | collective-permute-start | bytes 196616 | tf_op jit(solution)/shard_map/ppermute | solution.py:76
  46.9 5.7 %collective-permute-start.24 = (bf16[8,32,128]{2,1,0:T(8,128)(2,1)S(1)}, bf16[8,32,128]{2,1,0:T(8,128)(2,1)S(1)}, u32[]{:S(2)}, u32[]{:S(2)}) collective-permute-start(bf16[8,32,128]{2,1,0:T(8,128)(2,1)S(1)} %get-tuple-element.138), channel_id=1, source_target_pairs={{0,1},{1,0},{2,3},{3,2},{4,5},{5,4},{6,7},{7,6},{8,9},{9,8},{10,11... | collective-permute-start | bytes 196616 | tf_op jit(solution)/shard_map/ppermute | solution.py:76
  48.2 4.4 %collective-permute-start.25 = (bf16[8,32,128]{2,1,0:T(8,128)(2,1)S(1)}, bf16[8,32,128]{2,1,0:T(8,128)(2,1)S(1)}, u32[]{:S(2)}, u32[]{:S(2)}) collective-permute-start(bf16[8,32,128]{2,1,0:T(8,128)(2,1)S(1)} %get-tuple-element.139), channel_id=1, source_target_pairs={{0,8},{1,2},{2,1},{3,4},{4,3},{5,6},{6,5},{7,15},{8,0},{9,10},{10,... | collective-permute-start | bytes 196616 | tf_op jit(solution)/shard_map/ppermute | solution.py:76
  49.2 3.3 %collective-permute-start.26 = (bf16[4,32,128]{2,1,0:T(8,128)(2,1)S(1)}, bf16[4,32,128]{2,1,0:T(8,128)(2,1)S(1)}, u32[]{:S(2)}, u32[]{:S(2)}) collective-permute-start(bf16[4,32,128]{2,1,0:T(8,128)(2,1)S(1)} %get-tuple-element.140), channel_id=1, source_target_pairs={{0,24},{1,25},{2,26},{3,27},{4,28},{5,29},{6,30},{7,31},{8,16},{9,... | collective-permute-start | bytes 98312 | tf_op jit(solution)/shard_map/ppermute | solution.py:76
  53.0 6.5 %collective-permute-start.28 = (bf16[8,32,128]{2,1,0:T(8,128)(2,1)S(1)}, bf16[8,32,128]{2,1,0:T(8,128)(2,1)S(1)}, u32[]{:S(2)}, u32[]{:S(2)}) collective-permute-start(bf16[8,32,128]{2,1,0:T(8,128)(2,1)S(1)} %get-tuple-element.152), channel_id=1, source_target_pairs={{0,1},{1,0},{2,3},{3,2},{4,5},{5,4},{6,7},{7,6},{8,9},{9,8},{10,11... | collective-permute-start | bytes 196616 | tf_op jit(solution)/shard_map/ppermute | solution.py:76
  55.4 4.1 %collective-permute-start.29 = (bf16[8,32,128]{2,1,0:T(8,128)(2,1)S(1)}, bf16[8,32,128]{2,1,0:T(8,128)(2,1)S(1)}, u32[]{:S(2)}, u32[]{:S(2)}) collective-permute-start(bf16[8,32,128]{2,1,0:T(8,128)(2,1)S(1)} %get-tuple-element.153), channel_id=1, source_target_pairs={{0,8},{1,2},{2,1},{3,4},{4,3},{5,6},{6,5},{7,15},{8,0},{9,10},{10,... | collective-permute-start | bytes 196616 | tf_op jit(solution)/shard_map/ppermute | solution.py:76
  (8 other events, 25.6 us)

commit v2 on v1

v2 whole, which is shorter than its diff:
```python
import functools

import jax
import jax.numpy as jnp
from jax import lax
from jax.experimental import pallas as pl
from jax.experimental.pallas import tpu as pltpu
from jax.sharding import PartitionSpec as P

DEG = 8
BATCH = 16
ORDER = (0, 1, 3, 2)
SMEM = pl.BlockSpec(memory_space=pltpu.SMEM)
VMEM = pl.BlockSpec(memory_space=pltpu.VMEM)
HBM = pl.BlockSpec(memory_space=pl.ANY)
F32, BF16, I32 = jnp.float32, jnp.bfloat16, jnp.int32


def dot(x, b):
    return lax.dot_general(x, b, (((1,), (0,)), ((), ())), preferred_element_type=F32)


def in_vmem(x):
    return pltpu.with_memory_space_constraint(x, pltpu.VMEM)


def in_hbm(x):
    return pltpu.with_memory_space_constraint(x, pltpu.HBM)


def in_smem(x):
    return pltpu.with_memory_space_constraint(x, pltpu.SMEM)


def divisor(n, most):
    return next(d for d in range(min(n, most), 0, -1) if n % d == 0)


def swaps():
    regions, subs = lax.axis_size("region"), lax.axis_size("sub")

    def route(mate):
        pairs = []
        for r in range(regions):
            for s in range(subs):
                m = mate(r, s)
                if m is not None:
                    pairs.append((r * subs + s, m[0] * subs + m[1]))
        return pairs

    def idle_sub(r, s):
        return (r ^ 1, s) if r ^ 1 < regions else None

    def sub_even(r, s):
        return (r, s ^ 1) if s ^ 1 < subs else idle_sub(r, s)

    def sub_odd(r, s):
        m = ((s - 1) ^ 1) + 1
        return (r, m) if s > 0 and m < subs else idle_sub(r, s)

    def reg_even(r, s):
        return (r ^ 1, s) if r ^ 1 < regions else None

    def reg_odd(r, s):
        m = ((r - 1) ^ 1) + 1
        if r > 0 and m < regions:
            return (m, s)
        return (regions - 1 - r, s) if regions % 2 == 0 else None

    return [route(f) for f in (sub_even, sub_odd, reg_even, reg_odd)]


def exchange(sends):
    routes = swaps()
    return [lax.ppermute(x, ("region", "sub"), routes[k]) for x, k in zip(sends, ORDER)]


class Layout:
    def __init__(self, rows, hs, hr):
        self.rows, self.hs, self.hr = rows, hs, hr
        self.halo = 2 * hs + 2 * hr
        self.starts = (0, hs, 2 * hs, 2 * hs + hr)
        self.counts = (hs, hs, hr, hr)
        self.loc = 0
        self.far = 3 * rows
        self.n_far = self.far + 2 * rows + BATCH
        self.size = self.n_far + 1
        self.tab = 0
        self.out = self.halo
        self.n_out = self.out + 2 * self.halo + BATCH
        self.out_size = self.n_out + 1

    def lists(self, refs):
        return [(ref, self.starts[k], self.counts[k]) for ref, k in zip(refs, ORDER)]


def pack(place, block, got):
    return place + block * 1024 + got * (1 << 20)


def unpack(code):
    return code & 1023, (code >> 10) & 1023, code >> 20


def send_row(lay, sub_ref, reg_ref, j):
    rp, sp = lax.axis_index("region") % 2, lax.axis_index("sub") % 2
    hs, hr = lay.hs, lay.hr
    if j < hs:
        row = sub_ref[0, 1 - sp, j]
    elif j < 2 * hs:
        row = sub_ref[0, sp, j - hs]
    elif j < 2 * hs + hr:
        row = reg_ref[0, 1 - rp, j - 2 * hs]
    else:
        row = reg_ref[0, rp, j - 2 * hs - hr]
    return jnp.maximum(row, 0)


def received_place(lay, slot):
    rp, sp = lax.axis_index("region") % 2, lax.axis_index("sub") % 2
    hs, hr = lay.hs, lay.hr
    o = slot - lay.rows
    sub_at = jnp.where(sp == 1, o, jnp.where(o < hs, o + hs, o - hs))
    q = o - 2 * hs
    reg_at = jnp.where(rp == 1, o, jnp.where(q < hr, o + hr, o - hr))
    return jnp.maximum(jnp.where(o < 2 * hs, sub_at, reg_at), 0)


def first_send_kernel(lay, first, sub_hbm, reg_hbm, slot_hbm, coeff_hbm, probes_hbm, blocks_hbm,
                      s0, s1, s2, s3, slot_ref, coeff_ref, out_info, ext_ref, raw_ref, probes, sub_ref, reg_ref, sems):
    pairs = (
        (sub_hbm, sub_ref),
        (reg_hbm, reg_ref),
        (slot_hbm, slot_ref),
        (probes_hbm, probes),
        (coeff_hbm, coeff_ref),
        (blocks_hbm.at[pl.ds(0, first)], raw_ref.at[pl.ds(0, first)]),
    )
    loads = [pltpu.make_async_copy(a, b, sems.at[n]) for n, (a, b) in enumerate(pairs)]
    for load in loads:
        load.start()
    for load in loads[:3]:
        load.wait()
    at = []
    out = jnp.int32(0)
    for j in range(lay.halo):
        row = send_row(lay, sub_ref, reg_ref, j)
        at.append(row * 128)
        out_info[lay.tab + j] = row
        for k in (1, 2):
            slot = slot_ref[k, row]
            out_info[lay.out + out] = pack(j, 3 * row + k, received_place(lay, slot))
            out = out + jnp.where(slot < lay.rows, 0, 1)
    for u in range(BATCH):
        out_info[lay.out + out + u] = pack(lay.halo, 0, 0)
    out_info[lay.n_out] = out
    loads[3].wait()
    for ref, start, count in lay.lists((s0, s1, s2, s3)):
        for j in range(count):
            ref[j] = probes[:, pl.ds(pl.multiple_of(at[start + j], 128), 128)]
    for i in range(lay.rows):
        ext_ref[i] = probes[:, i * 128:(i + 1) * 128]
    ext_ref[lay.rows] = jnp.zeros_like(ext_ref[lay.rows])
    for load in loads[4:]:
        load.wait()


def prologue_kernel(lay, chunk, slot_ref, ext_ref, raw_in, blocks_hbm, bt_ref, y_ref, raw, info_ref, sems):
    del raw_in
    rows = lay.rows
    chunks = rows // chunk

    def load(c):
        part = pl.ds(c * chunk, chunk)
        return pltpu.make_async_copy(blocks_hbm.at[part], raw.at[part], sems.at[c])

    for c in range(1, chunks):
        load(c).start()
    y_ref[rows] = jnp.zeros_like(y_ref[rows])

    def many(c, far):
        @pl.when(c > 0)
        def _():
            load(c).wait()

        for u in range(chunk):
            i = c * chunk + u
            at = []
            for k in range(3):
                slot = slot_ref[k, i]
                at.append(jnp.where(slot < rows, slot, rows))
                info_ref[lay.loc + 3 * i + k] = at[k]
                if k > 0:
                    info_ref[lay.far + far] = pack(i, 3 * i + k, received_place(lay, slot))
                    far = far + jnp.where(slot < rows, 0, 1)
            turned = [raw[i, k].T for k in range(3)]
            for k in range(3):
                bt_ref[3 * i + k] = turned[k]
            x = jnp.concatenate([ext_ref[at[k]] for k in range(3)], 1)
            y_ref[i] = dot(x, jnp.concatenate(turned, 0))
        return far

    far = lax.fori_loop(0, chunks, many, jnp.int32(0))
    for u in range(BATCH):
        info_ref[lay.far + far + u] = pack(rows, 0, 0)
    info_ref[lay.n_far] = far


def gather_received(lay, got_refs, got):
    for ref, start, count in lay.lists(got_refs):
        for j in range(count):
            got[start + j] = ref[j]


def add_received(factor, info_ref, at, count, bt_ref, got, sum_ref):
    def batch(b, carry):
        found = []
        for u in range(BATCH):
            place, block, source = unpack(info_ref[at + b * BATCH + u])
            found.append((place, dot(got[source], bt_ref[block])))
        for place, value in found:
            sum_ref[place] += factor * value
        return carry

    lax.fori_loop(0, (count + BATCH - 1) // BATCH, batch, 0)


def send_kernel(lay, factor, info_ref, bt_ref, y_ref, g0, g1, g2, g3, y_out, s0, s1, s2, s3, got, held):
    del y_out
    gather_received(lay, (g0, g1, g2, g3), got)
    for j in range(lay.halo):
        held[j] = y_ref[info_ref[lay.tab + j]]
    add_received(factor, info_ref, lay.out, info_ref[lay.n_out], bt_ref, got, held)
    for ref, start, count in lay.lists((s0, s1, s2, s3)):
        for j in range(count):
            ref[j] = held[start + j].astype(BF16)


def step_kernel(lay, step, unroll, info_ref, coeff_ref, bt_ref, g0, g1, g2, g3, *refs):
    rows = lay.rows
    first, last = step == 1, step == DEG - 1
    if first:
        y_in, p_ref, x_ref, y_ref, t_ref, ext_ref, got = refs
    else:
        x_in, y_in, t_in, ext_in, x_ref, y_ref, t_ref, ext_ref, got = refs
    del y_in
    factor = 1.0 if first else 2.0
    gather_received(lay, (g0, g1, g2, g3), got)
    add_received(factor, info_ref, lay.far, info_ref[lay.n_far], bt_ref, got, y_ref)
    for i in range(rows):
        ext_ref[i] = y_ref[i].astype(BF16)
    if first:
        ext_ref[rows] = jnp.zeros_like(ext_ref[rows])
        t_ref[rows] = jnp.zeros_like(t_ref[rows])
        x_ref[rows] = jnp.zeros_like(x_ref[rows])
    c = coeff_ref[step]

    def many(j, carry):
        for u in range(unroll):
            i = j * unroll + u
            x = jnp.concatenate([ext_ref[info_ref[lay.loc + 3 * i + k]] for k in range(3)], 1)
            local = dot(x, bt_ref[pl.ds(3 * i, 3)].reshape(3 * 128, 128))
            if first:
                old = p_ref[i].astype(F32)
                t_ref[i] = coeff_ref[0] * old + c * y_ref[i]
                x_ref[i] = 2.0 * local - old
            elif last:
                t_ref[i] += c * y_ref[i] + coeff_ref[DEG] * (2.0 * local - x_ref[i])
            else:
                t_ref[i] += c * y_ref[i]
                x_ref[i] = 2.0 * local - x_ref[i]
        return carry

    lax.fori_loop(0, rows // unroll, many, 0)


def final_kernel(lay, part, info_ref, coeff_ref, bt_ref, t_in, g0, g1, g2, g3, out_hbm, t_ref, got, wide, sems):
    del t_in
    gather_received(lay, (g0, g1, g2, g3), got)
    add_received(2.0 * coeff_ref[DEG], info_ref, lay.far, info_ref[lay.n_far], bt_ref, got, t_ref)
    copies = []
    for j in range(lay.rows // part):
        for i in range(j * part, (j + 1) * part):
            wide[:, i * 128:(i + 1) * 128] = t_ref[i]
        columns = pl.ds(j * part * 128, part * 128)
        copies.append(pltpu.make_async_copy(wide.at[:, columns], out_hbm.at[:, columns], sems.at[j]))
        copies[-1].start()
    for copy in copies:
        copy.wait()


def local(probes, blocks, col_slot, send_sub, send_reg, coeffs):
    rows, _, width, _ = blocks.shape
    count = probes.shape[0]
    lay = Layout(rows, send_sub.shape[2], send_reg.shape[2])
    unroll = divisor(rows, 52)
    small = 4 << 20

    sends_shape = [pltpu.VMEM((n, count, width), BF16) for n in lay.counts]
    sends_shape = [sends_shape[k] for k in ORDER]
    got_scratch = pltpu.VMEM((lay.halo, count, width), BF16)
    state = pltpu.VMEM((rows + 1, count, width), F32)

    slots = col_slot.T
    chunk = divisor(rows, 26)
    part = divisor(rows, 26)
    ext_shape = pltpu.VMEM((rows + 1, count, width), BF16)
    results = pl.pallas_call(
        functools.partial(first_send_kernel, lay, chunk),
        in_specs=[HBM] * 6,
        out_specs=[VMEM] * 4 + [SMEM] * 3 + [VMEM] * 2,
        out_shape=sends_shape + [
            pltpu.SMEM(slots.shape, I32),
            pltpu.SMEM(coeffs.shape, F32),
            pltpu.SMEM((lay.out_size,), I32),
            ext_shape,
            pltpu.VMEM(blocks.shape, BF16),
        ],
        scratch_shapes=[
            pltpu.VMEM(probes.shape, BF16),
            pltpu.SMEM(send_sub.shape, I32),
            pltpu.SMEM(send_reg.shape, I32),
            pltpu.SemaphoreType.DMA((6,)),
        ],
        compiler_params=pltpu.CompilerParams(vmem_limit_bytes=small),
        name="first_send",
    )(*[in_hbm(a) for a in (send_sub, send_reg, slots, coeffs, probes, blocks)])
    sends, (slots, coeffs, out_info, start, raw0) = results[:4], results[4:]
    coeffs = in_smem(coeffs)
    got = exchange(sends)
    bt, y, _, info = pl.pallas_call(
        functools.partial(prologue_kernel, lay, chunk),
        in_specs=[SMEM] + [VMEM] * 2 + [HBM],
        out_specs=[VMEM] * 3 + [SMEM],
        out_shape=[
            pltpu.VMEM((3 * rows, width, width), BF16),
            state,
            pltpu.VMEM(blocks.shape, BF16),
            pltpu.SMEM((lay.size,), I32),
        ],
        scratch_shapes=[pltpu.SemaphoreType.DMA((rows // chunk,))],
        input_output_aliases={2: 2},
        compiler_params=pltpu.CompilerParams(vmem_limit_bytes=small),
        name="prologue",
    )(in_smem(slots), in_vmem(start), in_vmem(raw0), in_hbm(blocks))
    info, bt = in_smem(info), in_vmem(bt)
    for step in range(1, DEG):
        y, *sends = pl.pallas_call(
            functools.partial(send_kernel, lay, 1.0 if step == 1 else 2.0),
            in_specs=[SMEM, VMEM, VMEM] + [VMEM] * 4,
            out_specs=[VMEM] * 5,
            out_shape=[state] + sends_shape,
            scratch_shapes=[got_scratch, pltpu.VMEM((lay.halo + 1, count, width), F32)],
            input_output_aliases={2: 0},
            compiler_params=pltpu.CompilerParams(vmem_limit_bytes=small),
            name="send",
        )(in_smem(out_info), bt, in_vmem(y), *[in_vmem(g) for g in got])
        later = exchange(sends)
        if step == 1:
            states, aliases = [y, start], {7: 1}
        else:
            states, aliases = [x, y, t, ext], {7: 0, 8: 1, 9: 2, 10: 3}
        x, y, t, ext = pl.pallas_call(
            functools.partial(step_kernel, lay, step, unroll),
            in_specs=[SMEM, SMEM, VMEM] + [VMEM] * (4 + len(states)),
            out_specs=[VMEM] * 4,
            out_shape=[state, state, state, ext_shape],
            scratch_shapes=[got_scratch],
            input_output_aliases=aliases,
            compiler_params=pltpu.CompilerParams(vmem_limit_bytes=small),
            cost_estimate=pl.CostEstimate(flops=2 * rows * 3 * width * width * count, bytes_accessed=1 << 20, transcendentals=0),
            name="step",
        )(info, coeffs, bt, *[in_vmem(g) for g in got], *[in_vmem(a) for a in states])
        x, y = y, x
        got = later
    out, _ = pl.pallas_call(
        functools.partial(final_kernel, lay, part),
        in_specs=[SMEM, SMEM, VMEM, VMEM] + [VMEM] * 4,
        out_specs=[HBM, VMEM],
        out_shape=[jax.ShapeDtypeStruct((count, rows * width), F32), state],
        scratch_shapes=[got_scratch, pltpu.VMEM((count, rows * width), F32), pltpu.SemaphoreType.DMA((rows // part,))],
        input_output_aliases={3: 1},
        compiler_params=pltpu.CompilerParams(vmem_limit_bytes=small),
        name="final",
    )(info, coeffs, bt, in_vmem(t), *[in_vmem(g) for g in got])
    return out


def solution(mesh):
    return jax.shard_map(
        local,
        mesh=mesh,
        in_specs=(
            P(None, ("region", "sub")),
            P(("region", "sub"), None, None, None),
            P(("region", "sub"), None),
            P(("region", "sub"), None, None),
            P(("region", "sub"), None, None),
            P(),
        ),
        out_specs=P(None, ("region", "sub")),
        check_vma=False,
    )
```

time: 61.3 us -> 60.8 us (level)
  waiting for transfers between devices: 2.16 us -> 0.33 us
  starting transfers between devices: 30.5 us -> 31.9 us
    ppermute x32, waiting for transfers between devices: 2.16 us -> 0.33 us  [exchange(): lax.ppermute(x, ('region', 'sub'), routes[k])]
    ppermute x32, starting transfers between devices: 30.5 us -> 31.9 us  [exchange(): lax.ppermute(x, ('region', 'sub'), routes[k])]
    pallas_call x3, Pallas kernels: 8.97 us -> 7.84 us  [the longest x1 4.27 us: local(): pl.pallas_call(functools.partial(prologue_kernel, lay, chunk), in_specs=[...]
    pallas_call x7, Pallas kernels: 16.9 us -> 17.6 us  [local(): pl.pallas_call(functools.partial(step_kernel, lay, step, unroll), in_spec...]
  transfers between devices with their start and end apart: 32 -> 32, of which waited for: 5 -> 1; matrix products, arithmetic and copies ran while one was open for 0% -> 0% of each run, Pallas kernels for 37% -> 36%
where the time goes in v2:
time: 60.8 us; the launch traced here: 60.6 us
  starting transfers between devices  31.9 us (52%)
  Pallas kernels  27.9 us (46%)
    ppermute x32, starting transfers between devices, exchange(): lax.ppermute(x, ('region', 'sub'), routes[k])  31.9 us
    pallas_call x7, Pallas kernels, local(): pl.pallas_call(functools.partial(step_kernel, lay, step, unroll), in_spec...  17.6 us
    pallas_call x1, Pallas kernels, local(): pl.pallas_call(functools.partial(prologue_kernel, lay, chunk), in_specs=[...  4.27 us
    pallas_call x7, Pallas kernels, local(): pl.pallas_call(functools.partial(send_kernel, lay, 1.0 if step == 1 else...  2.51 us
    pallas_call x1, Pallas kernels, local(): pl.pallas_call(functools.partial(first_send_kernel, lay, chunk), in_specs...  2.04 us
    pallas_call x1, Pallas kernels, local(): pl.pallas_call(functools.partial(final_kernel, lay, part), in_specs=[SMEM...  1.53 us
  transfers between devices with their start and end apart: 32, of which 1 were waited for; matrix products, arithmetic and copies ran while one was open for 0% of the time, Pallas kernels for 36%

profile of v2, /device:TPU:1, one launch (start us, length us, event | category | flops | bytes accessed | tf_op | source)
XLA Modules:
  0.0 60.6 jit_solution(10409650358534434194)
XLA Ops:
  0.0 2.0 %first_send.1 = (bf16[8,32,128]{2,1,0:T(8,128)(2,1)S(1)}, bf16[8,32,128]{2,1,0:T(8,128)(2,1)S(1)}, bf16[4,32,128]{2,1,0:T(8,128)(2,1)S(1)}, bf16[4,32,128]{2,1,0...) custom-call(s32[1,2,8]{2,1,0:T(2,128)} %sub_hbm.1, ...), custom_call_target="tpu_custom_call" | custom-call | tf_op jit(solution)/shard_map/first_send/pallas_call | solution.py:308
  2.1 2.1 %collective-permute-start = (bf16[8,32,128]{2,1,0:T(8,128)(2,1)S(1)}, bf16[8,32,128]{2,1,0:T(8,128)(2,1)S(1)}, u32[]{:S(2)}, u32[]{:S(2)}) collective-permute-start(bf16[8,32,128]{2,1,0:T(8,128)(2,1)S(1)} %get-tuple-element.85), channel_id=1, source_target_pairs={{0,1},{1,0},{2,3},{3,2},{4,5},{5,4},{6,7},{7,6},{8,9},{9,8},{10,11... | collective-permute-start | bytes 196616 | tf_op jit(solution)/shard_map/ppermute | solution.py:75
  4.2 1.0 %collective-permute-start.1 = (bf16[8,32,128]{2,1,0:T(8,128)(2,1)S(1)}, bf16[8,32,128]{2,1,0:T(8,128)(2,1)S(1)}, u32[]{:S(2)}, u32[]{:S(2)}) collective-permute-start(bf16[8,32,128]{2,1,0:T(8,128)(2,1)S(1)} %get-tuple-element.86), channel_id=1, source_target_pairs={{0,8},{1,2},{2,1},{3,4},{4,3},{5,6},{6,5},{7,15},{8,0},{9,10},{10,... | collective-permute-start | bytes 196616 | tf_op jit(solution)/shard_map/ppermute | solution.py:75
  5.1 1.1 %collective-permute-start.2 = (bf16[4,32,128]{2,1,0:T(8,128)(2,1)S(1)}, bf16[4,32,128]{2,1,0:T(8,128)(2,1)S(1)}, u32[]{:S(2)}, u32[]{:S(2)}) collective-permute-start(bf16[4,32,128]{2,1,0:T(8,128)(2,1)S(1)} %get-tuple-element.87), channel_id=1, source_target_pairs={{0,24},{1,25},{2,26},{3,27},{4,28},{5,29},{6,30},{7,31},{8,16},{9,... | collective-permute-start | bytes 98312 | tf_op jit(solution)/shard_map/ppermute | solution.py:75
  6.8 4.3 %prologue.1 = (bf16[312,128,128]{2,1,0:T(8,128)(2,1)S(1)}, f32[105,32,128]{2,1,0:T(8,128)S(1)}, bf16[104,3,128,128]{3,2,1,0:T(8,128)(2,1)S(1)}, s32[537]{0:T(1024)S(4)}) custom-call(s32[3,104]{1,0:T(4,128)S(4)} %get-tuple-element.78.slot_ref, bf16[105,32,128]{2,1,0:T(8,128)(2,1)S(1)} %get-tuple-element.79.ext_ref.refs_1_, ...), custom_call_target="tpu_custom_call", output_to_operand_aliasing={{2}: (2, {})} | custom-call | tf_op jit(solution)/shard_map/prologue/pallas_call | solution.py:331
  11.4 2.3 %collective-permute-start.4 = (bf16[8,32,128]{2,1,0:T(8,128)(2,1)S(1)}, bf16[8,32,128]{2,1,0:T(8,128)(2,1)S(1)}, u32[]{:S(2)}, u32[]{:S(2)}) collective-permute-start(bf16[8,32,128]{2,1,0:T(8,128)(2,1)S(1)} %get-tuple-element.92), channel_id=1, source_target_pairs={{0,1},{1,0},{2,3},{3,2},{4,5},{5,4},{6,7},{7,6},{8,9},{9,8},{10,11... | collective-permute-start | bytes 196616 | tf_op jit(solution)/shard_map/ppermute | solution.py:75
  15.1 2.5 %step.7 = (f32[105,32,128]{2,1,0:T(8,128)S(1)}, f32[105,32,128]{2,1,0:T(8,128)S(1)}, f32[105,32,128]{2,1,0:T(8,128)S(1)}, bf16[105,32,128]{2,1,0:T(8,128)(2,1)S(1)}) custom-call(s32[537]{0:T(1024)S(4)} %get-tuple-element.81.info_ref, f32[9]{0:T(128)S(4)} %get-tuple-element.82.coeff_ref, ...), custom_call_target="tpu_custom_call", output_to_operand_aliasing={{1}: (7, {})} | custom-call | flops 327155712 | bytes 1048576 | tf_op jit(solution)/shard_map/step/pallas_call | solution.py:363
  18.2 2.0 %collective-permute-start.8 = (bf16[8,32,128]{2,1,0:T(8,128)(2,1)S(1)}, bf16[8,32,128]{2,1,0:T(8,128)(2,1)S(1)}, u32[]{:S(2)}, u32[]{:S(2)}) collective-permute-start(bf16[8,32,128]{2,1,0:T(8,128)(2,1)S(1)} %get-tuple-element.96), channel_id=1, source_target_pairs={{0,1},{1,0},{2,3},{3,2},{4,5},{5,4},{6,7},{7,6},{8,9},{9,8},{10,11... | collective-permute-start | bytes 196616 | tf_op jit(solution)/shard_map/ppermute | solution.py:75
  20.2 1.1 %collective-permute-start.9 = (bf16[8,32,128]{2,1,0:T(8,128)(2,1)S(1)}, bf16[8,32,128]{2,1,0:T(8,128)(2,1)S(1)}, u32[]{:S(2)}, u32[]{:S(2)}) collective-permute-start(bf16[8,32,128]{2,1,0:T(8,128)(2,1)S(1)} %get-tuple-element.97), channel_id=1, source_target_pairs={{0,8},{1,2},{2,1},{3,4},{4,3},{5,6},{6,5},{7,15},{8,0},{9,10},{10,... | collective-permute-start | bytes 196616 | tf_op jit(solution)/shard_map/ppermute | solution.py:75
  21.3 1.2 %collective-permute-start.10 = (bf16[4,32,128]{2,1,0:T(8,128)(2,1)S(1)}, bf16[4,32,128]{2,1,0:T(8,128)(2,1)S(1)}, u32[]{:S(2)}, u32[]{:S(2)}) collective-permute-start(bf16[4,32,128]{2,1,0:T(8,128)(2,1)S(1)} %get-tuple-element.98), channel_id=1, source_target_pairs={{0,24},{1,25},{2,26},{3,27},{4,28},{5,29},{6,30},{7,31},{8,16},{9,... | collective-permute-start | bytes 98312 | tf_op jit(solution)/shard_map/ppermute | solution.py:75
  23.0 2.5 %step.8 = (f32[105,32,128]{2,1,0:T(8,128)S(1)}, f32[105,32,128]{2,1,0:T(8,128)S(1)}, f32[105,32,128]{2,1,0:T(8,128)S(1)}, bf16[105,32,128]{2,1,0:T(8,128)(2,1)S(1)}) custom-call(s32[537]{0:T(1024)S(4)} %get-tuple-element.81.info_ref, f32[9]{0:T(128)S(4)} %get-tuple-element.82.coeff_ref, ...), custom_call_target="tpu_custom_call", output_to_operand_aliasing={{0}: (7, {}), {1}: (8, {}), {2}: (9, {}), {3}: (10, {})} | custom-call | flops 327155712 | bytes 1048576 | tf_op jit(solution)/shard_map/step/pallas_call | solution.py:363
  25.9 1.8 %collective-permute-start.12 = (bf16[8,32,128]{2,1,0:T(8,128)(2,1)S(1)}, bf16[8,32,128]{2,1,0:T(8,128)(2,1)S(1)}, u32[]{:S(2)}, u32[]{:S(2)}) collective-permute-start(bf16[8,32,128]{2,1,0:T(8,128)(2,1)S(1)} %get-tuple-element.110), channel_id=1, source_target_pairs={{0,1},{1,0},{2,3},{3,2},{4,5},{5,4},{6,7},{7,6},{8,9},{9,8},{10,11... | collective-permute-start | bytes 196616 | tf_op jit(solution)/shard_map/ppermute | solution.py:75
  28.5 0.9 %collective-permute-start.14 = (bf16[4,32,128]{2,1,0:T(8,128)(2,1)S(1)}, bf16[4,32,128]{2,1,0:T(8,128)(2,1)S(1)}, u32[]{:S(2)}, u32[]{:S(2)}) collective-permute-start(bf16[4,32,128]{2,1,0:T(8,128)(2,1)S(1)} %get-tuple-element.112), channel_id=1, source_target_pairs={{0,24},{1,25},{2,26},{3,27},{4,28},{5,29},{6,30},{7,31},{8,16},{9,... | collective-permute-start | bytes 98312 | tf_op jit(solution)/shard_map/ppermute | solution.py:75
  29.8 2.5 %step.9 = (f32[105,32,128]{2,1,0:T(8,128)S(1)}, f32[105,32,128]{2,1,0:T(8,128)S(1)}, f32[105,32,128]{2,1,0:T(8,128)S(1)}, bf16[105,32,128]{2,1,0:T(8,128)(2,1)S(1)}) custom-call(s32[537]{0:T(1024)S(4)} %get-tuple-element.81.info_ref, f32[9]{0:T(128)S(4)} %get-tuple-element.82.coeff_ref, ...), custom_call_target="tpu_custom_call", output_to_operand_aliasing={{0}: (7, {}), {1}: (8, {}), {2}: (9, {}), {3}: (10, {})} | custom-call | flops 327155712 | bytes 1048576 | tf_op jit(solution)/shard_map/step/pallas_call | solution.py:363
  32.7 1.1 %collective-permute-start.16 = (bf16[8,32,128]{2,1,0:T(8,128)(2,1)S(1)}, bf16[8,32,128]{2,1,0:T(8,128)(2,1)S(1)}, u32[]{:S(2)}, u32[]{:S(2)}) collective-permute-start(bf16[8,32,128]{2,1,0:T(8,128)(2,1)S(1)} %get-tuple-element.114), channel_id=1, source_target_pairs={{0,1},{1,0},{2,3},{3,2},{4,5},{5,4},{6,7},{7,6},{8,9},{9,8},{10,11... | collective-permute-start | bytes 196616 | tf_op jit(solution)/shard_map/ppermute | solution.py:75
  34.6 0.8 %collective-permute-start.18 = (bf16[4,32,128]{2,1,0:T(8,128)(2,1)S(1)}, bf16[4,32,128]{2,1,0:T(8,128)(2,1)S(1)}, u32[]{:S(2)}, u32[]{:S(2)}) collective-permute-start(bf16[4,32,128]{2,1,0:T(8,128)(2,1)S(1)} %get-tuple-element.116), channel_id=1, source_target_pairs={{0,24},{1,25},{2,26},{3,27},{4,28},{5,29},{6,30},{7,31},{8,16},{9,... | collective-permute-start | bytes 98312 | tf_op jit(solution)/shard_map/ppermute | solution.py:75
  35.9 2.5 %step.10 = (f32[105,32,128]{2,1,0:T(8,128)S(1)}, f32[105,32,128]{2,1,0:T(8,128)S(1)}, f32[105,32,128]{2,1,0:T(8,128)S(1)}, bf16[105,32,128]{2,1,0:T(8,128)(2,1)S(1)}) custom-call(s32[537]{0:T(1024)S(4)} %get-tuple-element.81.info_ref, f32[9]{0:T(128)S(4)} %get-tuple-element.82.coeff_ref, ...), custom_call_target="tpu_custom_call", output_to_operand_aliasing={{0}: (7, {}), {1}: (8, {}), {2}: (9, {}), {3}: (10, {})} | custom-call | flops 327155712 | bytes 1048576 | tf_op jit(solution)/shard_map/step/pallas_call | solution.py:363
  38.8 2.1 %collective-permute-start.20 = (bf16[8,32,128]{2,1,0:T(8,128)(2,1)S(1)}, bf16[8,32,128]{2,1,0:T(8,128)(2,1)S(1)}, u32[]{:S(2)}, u32[]{:S(2)}) collective-permute-start(bf16[8,32,128]{2,1,0:T(8,128)(2,1)S(1)} %get-tuple-element.128), channel_id=1, source_target_pairs={{0,1},{1,0},{2,3},{3,2},{4,5},{5,4},{6,7},{7,6},{8,9},{9,8},{10,11... | collective-permute-start | bytes 196616 | tf_op jit(solution)/shard_map/ppermute | solution.py:75
  43.0 2.5 %step.11 = (f32[105,32,128]{2,1,0:T(8,128)S(1)}, f32[105,32,128]{2,1,0:T(8,128)S(1)}, f32[105,32,128]{2,1,0:T(8,128)S(1)}, bf16[105,32,128]{2,1,0:T(8,128)(2,1)S(1)}) custom-call(s32[537]{0:T(1024)S(4)} %get-tuple-element.81.info_ref, f32[9]{0:T(128)S(4)} %get-tuple-element.82.coeff_ref, ...), custom_call_target="tpu_custom_call", output_to_operand_aliasing={{0}: (7, {}), {1}: (8, {}), {2}: (9, {}), {3}: (10, {})} | custom-call | flops 327155712 | bytes 1048576 | tf_op jit(solution)/shard_map/step/pallas_call | solution.py:363
  46.1 1.1 %collective-permute-start.24 = (bf16[8,32,128]{2,1,0:T(8,128)(2,1)S(1)}, bf16[8,32,128]{2,1,0:T(8,128)(2,1)S(1)}, u32[]{:S(2)}, u32[]{:S(2)}) collective-permute-start(bf16[8,32,128]{2,1,0:T(8,128)(2,1)S(1)} %get-tuple-element.132), channel_id=1, source_target_pairs={{0,1},{1,0},{2,3},{3,2},{4,5},{5,4},{6,7},{7,6},{8,9},{9,8},{10,11... | collective-permute-start | bytes 196616 | tf_op jit(solution)/shard_map/ppermute | solution.py:75
  49.2 2.5 %step.12 = (f32[105,32,128]{2,1,0:T(8,128)S(1)}, f32[105,32,128]{2,1,0:T(8,128)S(1)}, f32[105,32,128]{2,1,0:T(8,128)S(1)}, bf16[105,32,128]{2,1,0:T(8,128)(2,1)S(1)}) custom-call(s32[537]{0:T(1024)S(4)} %get-tuple-element.81.info_ref, f32[9]{0:T(128)S(4)} %get-tuple-element.82.coeff_ref, ...), custom_call_target="tpu_custom_call", output_to_operand_aliasing={{0}: (7, {}), {1}: (8, {}), {2}: (9, {}), {3}: (10, {})} | custom-call | flops 327155712 | bytes 1048576 | tf_op jit(solution)/shard_map/step/pallas_call | solution.py:363
  52.1 2.1 %collective-permute-start.28 = (bf16[8,32,128]{2,1,0:T(8,128)(2,1)S(1)}, bf16[8,32,128]{2,1,0:T(8,128)(2,1)S(1)}, u32[]{:S(2)}, u32[]{:S(2)}) collective-permute-start(bf16[8,32,128]{2,1,0:T(8,128)(2,1)S(1)} %get-tuple-element.146), channel_id=1, source_target_pairs={{0,1},{1,0},{2,3},{3,2},{4,5},{5,4},{6,7},{7,6},{8,9},{9,8},{10,11... | collective-permute-start | bytes 196616 | tf_op jit(solution)/shard_map/ppermute | solution.py:75
  56.3 2.6 %step.13 = (f32[105,32,128]{2,1,0:T(8,128)S(1)}, f32[105,32,128]{2,1,0:T(8,128)S(1)}, f32[105,32,128]{2,1,0:T(8,128)S(1)}, bf16[105,32,128]{2,1,0:T(8,128)(2,1)S(1)}) custom-call(s32[537]{0:T(1024)S(4)} %get-tuple-element.81.info_ref, f32[9]{0:T(128)S(4)} %get-tuple-element.82.coeff_ref, ...), custom_call_target="tpu_custom_call", output_to_operand_aliasing={{0}: (7, {}), {1}: (8, {}), {2}: (9, {}), {3}: (10, {})} | custom-call | flops 327155712 | bytes 1048576 | tf_op jit(solution)/shard_map/step/pallas_call | solution.py:363
  58.9 1.5 %final.1 = (f32[32,13312]{1,0:T(8,128)}, f32[105,32,128]{2,1,0:T(8,128)S(1)}) custom-call(s32[537]{0:T(1024)S(4)} %get-tuple-element.81.info_ref, f32[9]{0:T(128)S(4)} %get-tuple-element.82.coeff_ref, bf16[312,128,128]{2,1,0:T(8,128)(2,1)S(1)} %get-tuple-element.83.bt_ref, ...), custom_call_target="tpu_custom_call", output_to_operand_aliasing={{1}: (3, {})} | custom-call | tf_op jit(solution)/shard_map/final/pallas_call | solution.py:376
  (57 shorter events, 14.1 us)
Async XLA Ops:
  2.1 9.0 %collective-permute-start = (bf16[8,32,128]{2,1,0:T(8,128)(2,1)S(1)}, bf16[8,32,128]{2,1,0:T(8,128)(2,1)S(1)}, u32[]{:S(2)}, u32[]{:S(2)}) collective-permute-start(bf16[8,32,128]{2,1,0:T(8,128)(2,1)S(1)} %get-tuple-element.85), channel_id=1, source_target_pairs={{0,1},{1,0},{2,3},{3,2},{4,5},{5,4},{6,7},{7,6},{8,9},{9,8},{10,11... | collective-permute-start | bytes 196616 | tf_op jit(solution)/shard_map/ppermute | solution.py:75
  4.2 6.9 %collective-permute-start.1 = (bf16[8,32,128]{2,1,0:T(8,128)(2,1)S(1)}, bf16[8,32,128]{2,1,0:T(8,128)(2,1)S(1)}, u32[]{:S(2)}, u32[]{:S(2)}) collective-permute-start(bf16[8,32,128]{2,1,0:T(8,128)(2,1)S(1)} %get-tuple-element.86), channel_id=1, source_target_pairs={{0,8},{1,2},{2,1},{3,4},{4,3},{5,6},{6,5},{7,15},{8,0},{9,10},{10,... | collective-permute-start | bytes 196616 | tf_op jit(solution)/shard_map/ppermute | solution.py:75
  5.1 5.9 %collective-permute-start.2 = (bf16[4,32,128]{2,1,0:T(8,128)(2,1)S(1)}, bf16[4,32,128]{2,1,0:T(8,128)(2,1)S(1)}, u32[]{:S(2)}, u32[]{:S(2)}) collective-permute-start(bf16[4,32,128]{2,1,0:T(8,128)(2,1)S(1)} %get-tuple-element.87), channel_id=1, source_target_pairs={{0,24},{1,25},{2,26},{3,27},{4,28},{5,29},{6,30},{7,31},{8,16},{9,... | collective-permute-start | bytes 98312 | tf_op jit(solution)/shard_map/ppermute | solution.py:75
  6.2 4.8 %collective-permute-start.3 = (bf16[4,32,128]{2,1,0:T(8,128)(2,1)S(1)}, bf16[4,32,128]{2,1,0:T(8,128)(2,1)S(1)}, u32[]{:S(2)}, u32[]{:S(2)}) collective-permute-start(bf16[4,32,128]{2,1,0:T(8,128)(2,1)S(1)} %get-tuple-element.88), channel_id=1, source_target_pairs={{0,8},{1,9},{2,10},{3,11},{4,12},{5,13},{6,14},{7,15},{8,0},{9,1},... | collective-permute-start | bytes 98312 | tf_op jit(solution)/shard_map/ppermute | solution.py:75
  11.4 6.5 %collective-permute-start.4 = (bf16[8,32,128]{2,1,0:T(8,128)(2,1)S(1)}, bf16[8,32,128]{2,1,0:T(8,128)(2,1)S(1)}, u32[]{:S(2)}, u32[]{:S(2)}) collective-permute-start(bf16[8,32,128]{2,1,0:T(8,128)(2,1)S(1)} %get-tuple-element.92), channel_id=1, source_target_pairs={{0,1},{1,0},{2,3},{3,2},{4,5},{5,4},{6,7},{7,6},{8,9},{9,8},{10,11... | collective-permute-start | bytes 196616 | tf_op jit(solution)/shard_map/ppermute | solution.py:75
  13.7 4.1 %collective-permute-start.5 = (bf16[8,32,128]{2,1,0:T(8,128)(2,1)S(1)}, bf16[8,32,128]{2,1,0:T(8,128)(2,1)S(1)}, u32[]{:S(2)}, u32[]{:S(2)}) collective-permute-start(bf16[8,32,128]{2,1,0:T(8,128)(2,1)S(1)} %get-tuple-element.93), channel_id=1, source_target_pairs={{0,8},{1,2},{2,1},{3,4},{4,3},{5,6},{6,5},{7,15},{8,0},{9,10},{10,... | collective-permute-start | bytes 196616 | tf_op jit(solution)/shard_map/ppermute | solution.py:75
  18.2 7.3 %collective-permute-start.8 = (bf16[8,32,128]{2,1,0:T(8,128)(2,1)S(1)}, bf16[8,32,128]{2,1,0:T(8,128)(2,1)S(1)}, u32[]{:S(2)}, u32[]{:S(2)}) collective-permute-start(bf16[8,32,128]{2,1,0:T(8,128)(2,1)S(1)} %get-tuple-element.96), channel_id=1, source_target_pairs={{0,1},{1,0},{2,3},{3,2},{4,5},{5,4},{6,7},{7,6},{8,9},{9,8},{10,11... | collective-permute-start | bytes 196616 | tf_op jit(solution)/shard_map/ppermute | solution.py:75
  20.2 5.3 %collective-permute-start.9 = (bf16[8,32,128]{2,1,0:T(8,128)(2,1)S(1)}, bf16[8,32,128]{2,1,0:T(8,128)(2,1)S(1)}, u32[]{:S(2)}, u32[]{:S(2)}) collective-permute-start(bf16[8,32,128]{2,1,0:T(8,128)(2,1)S(1)} %get-tuple-element.97), channel_id=1, source_target_pairs={{0,8},{1,2},{2,1},{3,4},{4,3},{5,6},{6,5},{7,15},{8,0},{9,10},{10,... | collective-permute-start | bytes 196616 | tf_op jit(solution)/shard_map/ppermute | solution.py:75
  21.3 4.2 %collective-permute-start.10 = (bf16[4,32,128]{2,1,0:T(8,128)(2,1)S(1)}, bf16[4,32,128]{2,1,0:T(8,128)(2,1)S(1)}, u32[]{:S(2)}, u32[]{:S(2)}) collective-permute-start(bf16[4,32,128]{2,1,0:T(8,128)(2,1)S(1)} %get-tuple-element.98), channel_id=1, source_target_pairs={{0,24},{1,25},{2,26},{3,27},{4,28},{5,29},{6,30},{7,31},{8,16},{9,... | collective-permute-start | bytes 98312 | tf_op jit(solution)/shard_map/ppermute | solution.py:75
  25.9 6.5 %collective-permute-start.12 = (bf16[8,32,128]{2,1,0:T(8,128)(2,1)S(1)}, bf16[8,32,128]{2,1,0:T(8,128)(2,1)S(1)}, u32[]{:S(2)}, u32[]{:S(2)}) collective-permute-start(bf16[8,32,128]{2,1,0:T(8,128)(2,1)S(1)} %get-tuple-element.110), channel_id=1, source_target_pairs={{0,1},{1,0},{2,3},{3,2},{4,5},{5,4},{6,7},{7,6},{8,9},{9,8},{10,11... | collective-permute-start | bytes 196616 | tf_op jit(solution)/shard_map/ppermute | solution.py:75
  27.7 4.7 %collective-permute-start.13 = (bf16[8,32,128]{2,1,0:T(8,128)(2,1)S(1)}, bf16[8,32,128]{2,1,0:T(8,128)(2,1)S(1)}, u32[]{:S(2)}, u32[]{:S(2)}) collective-permute-start(bf16[8,32,128]{2,1,0:T(8,128)(2,1)S(1)} %get-tuple-element.111), channel_id=1, source_target_pairs={{0,8},{1,2},{2,1},{3,4},{4,3},{5,6},{6,5},{7,15},{8,0},{9,10},{10,... | collective-permute-start | bytes 196616 | tf_op jit(solution)/shard_map/ppermute | solution.py:75
  28.5 3.9 %collective-permute-start.14 = (bf16[4,32,128]{2,1,0:T(8,128)(2,1)S(1)}, bf16[4,32,128]{2,1,0:T(8,128)(2,1)S(1)}, u32[]{:S(2)}, u32[]{:S(2)}) collective-permute-start(bf16[4,32,128]{2,1,0:T(8,128)(2,1)S(1)} %get-tuple-element.112), channel_id=1, source_target_pairs={{0,24},{1,25},{2,26},{3,27},{4,28},{5,29},{6,30},{7,31},{8,16},{9,... | collective-permute-start | bytes 98312 | tf_op jit(solution)/shard_map/ppermute | solution.py:75
  32.7 5.7 %collective-permute-start.16 = (bf16[8,32,128]{2,1,0:T(8,128)(2,1)S(1)}, bf16[8,32,128]{2,1,0:T(8,128)(2,1)S(1)}, u32[]{:S(2)}, u32[]{:S(2)}) collective-permute-start(bf16[8,32,128]{2,1,0:T(8,128)(2,1)S(1)} %get-tuple-element.114), channel_id=1, source_target_pairs={{0,1},{1,0},{2,3},{3,2},{4,5},{5,4},{6,7},{7,6},{8,9},{9,8},{10,11... | collective-permute-start | bytes 196616 | tf_op jit(solution)/shard_map/ppermute | solution.py:75
  33.8 4.7 %collective-permute-start.17 = (bf16[8,32,128]{2,1,0:T(8,128)(2,1)S(1)}, bf16[8,32,128]{2,1,0:T(8,128)(2,1)S(1)}, u32[]{:S(2)}, u32[]{:S(2)}) collective-permute-start(bf16[8,32,128]{2,1,0:T(8,128)(2,1)S(1)} %get-tuple-element.115), channel_id=1, source_target_pairs={{0,8},{1,2},{2,1},{3,4},{4,3},{5,6},{6,5},{7,15},{8,0},{9,10},{10,... | collective-permute-start | bytes 196616 | tf_op jit(solution)/shard_map/ppermute | solution.py:75
  34.6 3.9 %collective-permute-start.18 = (bf16[4,32,128]{2,1,0:T(8,128)(2,1)S(1)}, bf16[4,32,128]{2,1,0:T(8,128)(2,1)S(1)}, u32[]{:S(2)}, u32[]{:S(2)}) collective-permute-start(bf16[4,32,128]{2,1,0:T(8,128)(2,1)S(1)} %get-tuple-element.116), channel_id=1, source_target_pairs={{0,24},{1,25},{2,26},{3,27},{4,28},{5,29},{6,30},{7,31},{8,16},{9,... | collective-permute-start | bytes 98312 | tf_op jit(solution)/shard_map/ppermute | solution.py:75
  38.8 6.7 %collective-permute-start.20 = (bf16[8,32,128]{2,1,0:T(8,128)(2,1)S(1)}, bf16[8,32,128]{2,1,0:T(8,128)(2,1)S(1)}, u32[]{:S(2)}, u32[]{:S(2)}) collective-permute-start(bf16[8,32,128]{2,1,0:T(8,128)(2,1)S(1)} %get-tuple-element.128), channel_id=1, source_target_pairs={{0,1},{1,0},{2,3},{3,2},{4,5},{5,4},{6,7},{7,6},{8,9},{9,8},{10,11... | collective-permute-start | bytes 196616 | tf_op jit(solution)/shard_map/ppermute | solution.py:75
  40.9 4.7 %collective-permute-start.21 = (bf16[8,32,128]{2,1,0:T(8,128)(2,1)S(1)}, bf16[8,32,128]{2,1,0:T(8,128)(2,1)S(1)}, u32[]{:S(2)}, u32[]{:S(2)}) collective-permute-start(bf16[8,32,128]{2,1,0:T(8,128)(2,1)S(1)} %get-tuple-element.129), channel_id=1, source_target_pairs={{0,8},{1,2},{2,1},{3,4},{4,3},{5,6},{6,5},{7,15},{8,0},{9,10},{10,... | collective-permute-start | bytes 196616 | tf_op jit(solution)/shard_map/ppermute | solution.py:75
  41.7 3.8 %collective-permute-start.22 = (bf16[4,32,128]{2,1,0:T(8,128)(2,1)S(1)}, bf16[4,32,128]{2,1,0:T(8,128)(2,1)S(1)}, u32[]{:S(2)}, u32[]{:S(2)}) collective-permute-start(bf16[4,32,128]{2,1,0:T(8,128)(2,1)S(1)} %get-tuple-element.130), channel_id=1, source_target_pairs={{0,24},{1,25},{2,26},{3,27},{4,28},{5,29},{6,30},{7,31},{8,16},{9,... | collective-permute-start | bytes 98312 | tf_op jit(solution)/shard_map/ppermute | solution.py:75
  46.1 5.7 %collective-permute-start.24 = (bf16[8,32,128]{2,1,0:T(8,128)(2,1)S(1)}, bf16[8,32,128]{2,1,0:T(8,128)(2,1)S(1)}, u32[]{:S(2)}, u32[]{:S(2)}) collective-permute-start(bf16[8,32,128]{2,1,0:T(8,128)(2,1)S(1)} %get-tuple-element.132), channel_id=1, source_target_pairs={{0,1},{1,0},{2,3},{3,2},{4,5},{5,4},{6,7},{7,6},{8,9},{9,8},{10,11... | collective-permute-start | bytes 196616 | tf_op jit(solution)/shard_map/ppermute | solution.py:75
  47.1 4.7 %collective-permute-start.25 = (bf16[8,32,128]{2,1,0:T(8,128)(2,1)S(1)}, bf16[8,32,128]{2,1,0:T(8,128)(2,1)S(1)}, u32[]{:S(2)}, u32[]{:S(2)}) collective-permute-start(bf16[8,32,128]{2,1,0:T(8,128)(2,1)S(1)} %get-tuple-element.133), channel_id=1, source_target_pairs={{0,8},{1,2},{2,1},{3,4},{4,3},{5,6},{6,5},{7,15},{8,0},{9,10},{10,... | collective-permute-start | bytes 196616 | tf_op jit(solution)/shard_map/ppermute | solution.py:75
  47.9 3.8 %collective-permute-start.26 = (bf16[4,32,128]{2,1,0:T(8,128)(2,1)S(1)}, bf16[4,32,128]{2,1,0:T(8,128)(2,1)S(1)}, u32[]{:S(2)}, u32[]{:S(2)}) collective-permute-start(bf16[4,32,128]{2,1,0:T(8,128)(2,1)S(1)} %get-tuple-element.134), channel_id=1, source_target_pairs={{0,24},{1,25},{2,26},{3,27},{4,28},{5,29},{6,30},{7,31},{8,16},{9,... | collective-permute-start | bytes 98312 | tf_op jit(solution)/shard_map/ppermute | solution.py:75
  52.1 6.8 %collective-permute-start.28 = (bf16[8,32,128]{2,1,0:T(8,128)(2,1)S(1)}, bf16[8,32,128]{2,1,0:T(8,128)(2,1)S(1)}, u32[]{:S(2)}, u32[]{:S(2)}) collective-permute-start(bf16[8,32,128]{2,1,0:T(8,128)(2,1)S(1)} %get-tuple-element.146), channel_id=1, source_target_pairs={{0,1},{1,0},{2,3},{3,2},{4,5},{5,4},{6,7},{7,6},{8,9},{9,8},{10,11... | collective-permute-start | bytes 196616 | tf_op jit(solution)/shard_map/ppermute | solution.py:75
  54.2 4.7 %collective-permute-start.29 = (bf16[8,32,128]{2,1,0:T(8,128)(2,1)S(1)}, bf16[8,32,128]{2,1,0:T(8,128)(2,1)S(1)}, u32[]{:S(2)}, u32[]{:S(2)}) collective-permute-start(bf16[8,32,128]{2,1,0:T(8,128)(2,1)S(1)} %get-tuple-element.147), channel_id=1, source_target_pairs={{0,8},{1,2},{2,1},{3,4},{4,3},{5,6},{6,5},{7,15},{8,0},{9,10},{10,... | collective-permute-start | bytes 196616 | tf_op jit(solution)/shard_map/ppermute | solution.py:75
  55.0 3.9 %collective-permute-start.30 = (bf16[4,32,128]{2,1,0:T(8,128)(2,1)S(1)}, bf16[4,32,128]{2,1,0:T(8,128)(2,1)S(1)}, u32[]{:S(2)}, u32[]{:S(2)}) collective-permute-start(bf16[4,32,128]{2,1,0:T(8,128)(2,1)S(1)} %get-tuple-element.148), channel_id=1, source_target_pairs={{0,24},{1,25},{2,26},{3,27},{4,28},{5,29},{6,30},{7,31},{8,16},{9,... | collective-permute-start | bytes 98312 | tf_op jit(solution)/shard_map/ppermute | solution.py:75
  (8 other events, 24.8 us)

commit v3 on v2

--- a/solution.py
+++ b/solution.py
@@ -126,15 +126,14 @@
     return jnp.maximum(jnp.where(o < 2 * hs, sub_at, reg_at), 0)
 
 
-def first_send_kernel(lay, first, sub_hbm, reg_hbm, slot_hbm, coeff_hbm, probes_hbm, blocks_hbm,
-                      s0, s1, s2, s3, slot_ref, coeff_ref, out_info, ext_ref, raw_ref, probes, sub_ref, reg_ref, sems):
+def first_send_kernel(lay, sub_hbm, reg_hbm, slot_hbm, coeff_hbm, probes_hbm,
+                      s0, s1, s2, s3, slot_ref, coeff_ref, out_info, ext_ref, probes, sub_ref, reg_ref, sems):
     pairs = (
         (sub_hbm, sub_ref),
         (reg_hbm, reg_ref),
         (slot_hbm, slot_ref),
         (probes_hbm, probes),
         (coeff_hbm, coeff_ref),
-        (blocks_hbm.at[pl.ds(0, first)], raw_ref.at[pl.ds(0, first)]),
     )
     loads = [pltpu.make_async_copy(a, b, sems.at[n]) for n, (a, b) in enumerate(pairs)]
     for load in loads:
@@ -165,24 +164,12 @@
         load.wait()
 
 
-def prologue_kernel(lay, chunk, slot_ref, ext_ref, raw_in, blocks_hbm, bt_ref, y_ref, raw, info_ref, sems):
-    del raw_in
+def prologue_kernel(lay, chunk, slot_ref, ext_ref, raw, bt_ref, y_ref, info_ref):
     rows = lay.rows
     chunks = rows // chunk
-
-    def load(c):
-        part = pl.ds(c * chunk, chunk)
-        return pltpu.make_async_copy(blocks_hbm.at[part], raw.at[part], sems.at[c])
-
-    for c in range(1, chunks):
-        load(c).start()
     y_ref[rows] = jnp.zeros_like(y_ref[rows])
 
     def many(c, far):
-        @pl.when(c > 0)
-        def _():
-            load(c).wait()
-
         for u in range(chunk):
             i = c * chunk + u
             at = []
@@ -306,43 +293,36 @@
     part = divisor(rows, 26)
     ext_shape = pltpu.VMEM((rows + 1, count, width), BF16)
     results = pl.pallas_call(
-        functools.partial(first_send_kernel, lay, chunk),
-        in_specs=[HBM] * 6,
-        out_specs=[VMEM] * 4 + [SMEM] * 3 + [VMEM] * 2,
+        functools.partial(first_send_kernel, lay),
+        in_specs=[HBM] * 5,
+        out_specs=[VMEM] * 4 + [SMEM] * 3 + [VMEM],
         out_shape=sends_shape + [
             pltpu.SMEM(slots.shape, I32),
             pltpu.SMEM(coeffs.shape, F32),
             pltpu.SMEM((lay.out_size,), I32),
             ext_shape,
-            pltpu.VMEM(blocks.shape, BF16),
         ],
         scratch_shapes=[
             pltpu.VMEM(probes.shape, BF16),
             pltpu.SMEM(send_sub.shape, I32),
             pltpu.SMEM(send_reg.shape, I32),
-            pltpu.SemaphoreType.DMA((6,)),
+            pltpu.SemaphoreType.DMA((5,)),
         ],
         compiler_params=pltpu.CompilerParams(vmem_limit_bytes=small),
+        cost_estimate=pl.CostEstimate(flops=10**10, bytes_accessed=60 << 20, transcendentals=0),
         name="first_send",
-    )(*[in_hbm(a) for a in (send_sub, send_reg, slots, coeffs, probes, blocks)])
-    sends, (slots, coeffs, out_info, start, raw0) = results[:4], results[4:]
+    )(*[in_hbm(a) for a in (send_sub, send_reg, slots, coeffs, probes)])
+    sends, (slots, coeffs, out_info, start) = results[:4], results[4:]
     coeffs = in_smem(coeffs)
     got = exchange(sends)
-    bt, y, _, info = pl.pallas_call(
+    bt, y, info = pl.pallas_call(
         functools.partial(prologue_kernel, lay, chunk),
-        in_specs=[SMEM] + [VMEM] * 2 + [HBM],
-        out_specs=[VMEM] * 3 + [SMEM],
-        out_shape=[
-            pltpu.VMEM((3 * rows, width, width), BF16),
-            state,
-            pltpu.VMEM(blocks.shape, BF16),
-            pltpu.SMEM((lay.size,), I32),
-        ],
-        scratch_shapes=[pltpu.SemaphoreType.DMA((rows // chunk,))],
-        input_output_aliases={2: 2},
-        compiler_params=pltpu.CompilerParams(vmem_limit_bytes=small),
+        in_specs=[SMEM] + [VMEM] * 2,
+        out_specs=[VMEM] * 2 + [SMEM],
+        out_shape=[pltpu.VMEM((3 * rows, width, width), BF16), state, pltpu.SMEM((lay.size,), I32)],
+        compiler_params=pltpu.CompilerParams(vmem_limit_bytes=28 << 20),
         name="prologue",
-    )(in_smem(slots), in_vmem(start), in_vmem(raw0), in_hbm(blocks))
+    )(in_smem(slots), in_vmem(start), blocks)
     info, bt = in_smem(info), in_vmem(bt)
     for step in range(1, DEG):
         y, *sends = pl.pallas_call(

time: 60.8 us -> 59.2 us (0.974)
  Pallas kernels: 27.9 us -> 25.7 us
  starting transfers between devices: 31.9 us -> 32.6 us
    pallas_call x1, Pallas kernels: 4.27 us -> 3.34 us  [local(): pl.pallas_call(functools.partial(prologue_kernel, lay, chunk), in_specs=[...]
    pallas_call x7, Pallas kernels: 17.6 us -> 16.8 us  [local(): pl.pallas_call(functools.partial(step_kernel, lay, step, unroll), in_spec...]
    ppermute x32, starting transfers between devices: 31.9 us -> 32.6 us  [exchange(): lax.ppermute(x, ('region', 'sub'), routes[k])]
  transfers between devices with their start and end apart: 32 -> 32, of which waited for: 1 -> 1; matrix products, arithmetic and copies ran while one was open for 0% -> 0% of each run, Pallas kernels for 36% -> 34%
where the time goes in v3:
time: 59.2 us
  starting transfers between devices  32.6 us (55%)
  Pallas kernels  25.7 us (43%)
    ppermute x32, starting transfers between devices, exchange(): lax.ppermute(x, ('region', 'sub'), routes[k])  32.6 us
    pallas_call x7, Pallas kernels, local(): pl.pallas_call(functools.partial(step_kernel, lay, step, unroll), in_spec...  16.8 us
    pallas_call x1, Pallas kernels, local(): pl.pallas_call(functools.partial(prologue_kernel, lay, chunk), in_specs=[...  3.34 us
    pallas_call x7, Pallas kernels, local(): pl.pallas_call(functools.partial(send_kernel, lay, 1.0 if step == 1 else...  2.51 us
    pallas_call x1, Pallas kernels, local(): pl.pallas_call(functools.partial(first_send_kernel, lay), in_specs=[HBM]...  1.59 us
    pallas_call x1, Pallas kernels, local(): pl.pallas_call(functools.partial(final_kernel, lay, part), in_specs=[SMEM...  1.53 us
  transfers between devices with their start and end apart: 32, of which 1 were waited for; matrix products, arithmetic and copies ran while one was open for 0% of the time, Pallas kernels for 34%

profile of v3, /device:TPU:1, one launch (start us, length us, event | category | flops | bytes accessed | tf_op | source)
XLA Modules:
  0.0 59.2 jit_solution(8208105993093968669)
XLA Ops:
  0.0 1.6 %first_send.1 = (bf16[8,32,128]{2,1,0:T(8,128)(2,1)S(1)}, bf16[8,32,128]{2,1,0:T(8,128)(2,1)S(1)}, bf16[4,32,128]{2,1,0:T(8,128)(2,1)S(1)}, bf16[4,32,128]{2,1,0...) custom-call(s32[1,2,8]{2,1,0:T(2,128)} %sub_hbm.1, ...), custom_call_target="tpu_custom_call" | custom-call | flops 10000000000 | bytes 62914560 | tf_op jit(solution)/shard_map/first_send/pallas_call | solution.py:295
  1.6 2.1 %collective-permute-start = (bf16[8,32,128]{2,1,0:T(8,128)(2,1)S(1)}, bf16[8,32,128]{2,1,0:T(8,128)(2,1)S(1)}, u32[]{:S(2)}, u32[]{:S(2)}) collective-permute-start(bf16[8,32,128]{2,1,0:T(8,128)(2,1)S(1)} %get-tuple-element.83), channel_id=1, source_target_pairs={{0,1},{1,0},{2,3},{3,2},{4,5},{5,4},{6,7},{7,6},{8,9},{9,8},{10,11... | collective-permute-start | bytes 196616 | tf_op jit(solution)/shard_map/ppermute | solution.py:75
  3.7 1.0 %collective-permute-start.1 = (bf16[8,32,128]{2,1,0:T(8,128)(2,1)S(1)}, bf16[8,32,128]{2,1,0:T(8,128)(2,1)S(1)}, u32[]{:S(2)}, u32[]{:S(2)}) collective-permute-start(bf16[8,32,128]{2,1,0:T(8,128)(2,1)S(1)} %get-tuple-element.84), channel_id=1, source_target_pairs={{0,8},{1,2},{2,1},{3,4},{4,3},{5,6},{6,5},{7,15},{8,0},{9,10},{10,... | collective-permute-start | bytes 196616 | tf_op jit(solution)/shard_map/ppermute | solution.py:75
  4.7 1.1 %collective-permute-start.2 = (bf16[4,32,128]{2,1,0:T(8,128)(2,1)S(1)}, bf16[4,32,128]{2,1,0:T(8,128)(2,1)S(1)}, u32[]{:S(2)}, u32[]{:S(2)}) collective-permute-start(bf16[4,32,128]{2,1,0:T(8,128)(2,1)S(1)} %get-tuple-element.85), channel_id=1, source_target_pairs={{0,24},{1,25},{2,26},{3,27},{4,28},{5,29},{6,30},{7,31},{8,16},{9,... | collective-permute-start | bytes 98312 | tf_op jit(solution)/shard_map/ppermute | solution.py:75
  6.3 3.3 %prologue.1 = (bf16[312,128,128]{2,1,0:T(8,128)(2,1)S(1)}, f32[105,32,128]{2,1,0:T(8,128)S(1)}, s32[537]{0:T(1024)S(4)}) custom-call(s32[3,104]{1,0:T(4,128)S(4)} %get-tuple-element.77.slot_ref, bf16[105,32,128]{2,1,0:T(8,128)(2,1)S(1)} %get-tuple-element.78.ext_ref.refs_1_, bf16[104,3,128,128]{3,2,1,0:T(8,128)(2,1)S(1)} %bitcast.2), custom_call_target="tpu_custom_call" | custom-call | tf_op jit(solution)/shard_map/prologue/pallas_call | solution.py:318
  10.0 2.3 %collective-permute-start.4 = (bf16[8,32,128]{2,1,0:T(8,128)(2,1)S(1)}, bf16[8,32,128]{2,1,0:T(8,128)(2,1)S(1)}, u32[]{:S(2)}, u32[]{:S(2)}) collective-permute-start(bf16[8,32,128]{2,1,0:T(8,128)(2,1)S(1)} %get-tuple-element.90), channel_id=1, source_target_pairs={{0,1},{1,0},{2,3},{3,2},{4,5},{5,4},{6,7},{7,6},{8,9},{9,8},{10,11... | collective-permute-start | bytes 196616 | tf_op jit(solution)/shard_map/ppermute | solution.py:75
  12.4 0.8 %collective-permute-start.5 = (bf16[8,32,128]{2,1,0:T(8,128)(2,1)S(1)}, bf16[8,32,128]{2,1,0:T(8,128)(2,1)S(1)}, u32[]{:S(2)}, u32[]{:S(2)}) collective-permute-start(bf16[8,32,128]{2,1,0:T(8,128)(2,1)S(1)} %get-tuple-element.91), channel_id=1, source_target_pairs={{0,8},{1,2},{2,1},{3,4},{4,3},{5,6},{6,5},{7,15},{8,0},{9,10},{10,... | collective-permute-start | bytes 196616 | tf_op jit(solution)/shard_map/ppermute | solution.py:75
  13.8 2.4 %step.7 = (f32[105,32,128]{2,1,0:T(8,128)S(1)}, f32[105,32,128]{2,1,0:T(8,128)S(1)}, f32[105,32,128]{2,1,0:T(8,128)S(1)}, bf16[105,32,128]{2,1,0:T(8,128)(2,1)S(1)}) custom-call(s32[537]{0:T(1024)S(4)} %get-tuple-element.79.info_ref, f32[9]{0:T(128)S(4)} %get-tuple-element.80.coeff_ref, ...), custom_call_target="tpu_custom_call", output_to_operand_aliasing={{1}: (7, {})} | custom-call | flops 327155712 | bytes 1048576 | tf_op jit(solution)/shard_map/step/pallas_call | solution.py:343
  16.8 2.2 %collective-permute-start.8 = (bf16[8,32,128]{2,1,0:T(8,128)(2,1)S(1)}, bf16[8,32,128]{2,1,0:T(8,128)(2,1)S(1)}, u32[]{:S(2)}, u32[]{:S(2)}) collective-permute-start(bf16[8,32,128]{2,1,0:T(8,128)(2,1)S(1)} %get-tuple-element.94), channel_id=1, source_target_pairs={{0,1},{1,0},{2,3},{3,2},{4,5},{5,4},{6,7},{7,6},{8,9},{9,8},{10,11... | collective-permute-start | bytes 196616 | tf_op jit(solution)/shard_map/ppermute | solution.py:75
  19.0 0.9 %collective-permute-start.9 = (bf16[8,32,128]{2,1,0:T(8,128)(2,1)S(1)}, bf16[8,32,128]{2,1,0:T(8,128)(2,1)S(1)}, u32[]{:S(2)}, u32[]{:S(2)}) collective-permute-start(bf16[8,32,128]{2,1,0:T(8,128)(2,1)S(1)} %get-tuple-element.95), channel_id=1, source_target_pairs={{0,8},{1,2},{2,1},{3,4},{4,3},{5,6},{6,5},{7,15},{8,0},{9,10},{10,... | collective-permute-start | bytes 196616 | tf_op jit(solution)/shard_map/ppermute | solution.py:75
  19.9 0.9 %collective-permute-start.10 = (bf16[4,32,128]{2,1,0:T(8,128)(2,1)S(1)}, bf16[4,32,128]{2,1,0:T(8,128)(2,1)S(1)}, u32[]{:S(2)}, u32[]{:S(2)}) collective-permute-start(bf16[4,32,128]{2,1,0:T(8,128)(2,1)S(1)} %get-tuple-element.96), channel_id=1, source_target_pairs={{0,24},{1,25},{2,26},{3,27},{4,28},{5,29},{6,30},{7,31},{8,16},{9,... | collective-permute-start | bytes 98312 | tf_op jit(solution)/shard_map/ppermute | solution.py:75
  21.3 2.4 %step.8 = (f32[105,32,128]{2,1,0:T(8,128)S(1)}, f32[105,32,128]{2,1,0:T(8,128)S(1)}, f32[105,32,128]{2,1,0:T(8,128)S(1)}, bf16[105,32,128]{2,1,0:T(8,128)(2,1)S(1)}) custom-call(s32[537]{0:T(1024)S(4)} %get-tuple-element.79.info_ref, f32[9]{0:T(128)S(4)} %get-tuple-element.80.coeff_ref, ...), custom_call_target="tpu_custom_call", output_to_operand_aliasing={{0}: (7, {}), {1}: (8, {}), {2}: (9, {}), {3}: (10, {})} | custom-call | flops 327155712 | bytes 1048576 | tf_op jit(solution)/shard_map/step/pallas_call | solution.py:343
  24.1 2.3 %collective-permute-start.12 = (bf16[8,32,128]{2,1,0:T(8,128)(2,1)S(1)}, bf16[8,32,128]{2,1,0:T(8,128)(2,1)S(1)}, u32[]{:S(2)}, u32[]{:S(2)}) collective-permute-start(bf16[8,32,128]{2,1,0:T(8,128)(2,1)S(1)} %get-tuple-element.108), channel_id=1, source_target_pairs={{0,1},{1,0},{2,3},{3,2},{4,5},{5,4},{6,7},{7,6},{8,9},{9,8},{10,11... | collective-permute-start | bytes 196616 | tf_op jit(solution)/shard_map/ppermute | solution.py:75
  28.1 2.4 %step.9 = (f32[105,32,128]{2,1,0:T(8,128)S(1)}, f32[105,32,128]{2,1,0:T(8,128)S(1)}, f32[105,32,128]{2,1,0:T(8,128)S(1)}, bf16[105,32,128]{2,1,0:T(8,128)(2,1)S(1)}) custom-call(s32[537]{0:T(1024)S(4)} %get-tuple-element.79.info_ref, f32[9]{0:T(128)S(4)} %get-tuple-element.80.coeff_ref, ...), custom_call_target="tpu_custom_call", output_to_operand_aliasing={{0}: (7, {}), {1}: (8, {}), {2}: (9, {}), {3}: (10, {})} | custom-call | flops 327155712 | bytes 1048576 | tf_op jit(solution)/shard_map/step/pallas_call | solution.py:343
  30.9 1.6 %collective-permute-start.16 = (bf16[8,32,128]{2,1,0:T(8,128)(2,1)S(1)}, bf16[8,32,128]{2,1,0:T(8,128)(2,1)S(1)}, u32[]{:S(2)}, u32[]{:S(2)}) collective-permute-start(bf16[8,32,128]{2,1,0:T(8,128)(2,1)S(1)} %get-tuple-element.112), channel_id=1, source_target_pairs={{0,1},{1,0},{2,3},{3,2},{4,5},{5,4},{6,7},{7,6},{8,9},{9,8},{10,11... | collective-permute-start | bytes 196616 | tf_op jit(solution)/shard_map/ppermute | solution.py:75
  34.2 2.4 %step.10 = (f32[105,32,128]{2,1,0:T(8,128)S(1)}, f32[105,32,128]{2,1,0:T(8,128)S(1)}, f32[105,32,128]{2,1,0:T(8,128)S(1)}, bf16[105,32,128]{2,1,0:T(8,128)(2,1)S(1)}) custom-call(s32[537]{0:T(1024)S(4)} %get-tuple-element.79.info_ref, f32[9]{0:T(128)S(4)} %get-tuple-element.80.coeff_ref, ...), custom_call_target="tpu_custom_call", output_to_operand_aliasing={{0}: (7, {}), {1}: (8, {}), {2}: (9, {}), {3}: (10, {})} | custom-call | flops 327155712 | bytes 1048576 | tf_op jit(solution)/shard_map/step/pallas_call | solution.py:343
  36.9 2.8 %collective-permute-start.20 = (bf16[8,32,128]{2,1,0:T(8,128)(2,1)S(1)}, bf16[8,32,128]{2,1,0:T(8,128)(2,1)S(1)}, u32[]{:S(2)}, u32[]{:S(2)}) collective-permute-start(bf16[8,32,128]{2,1,0:T(8,128)(2,1)S(1)} %get-tuple-element.126), channel_id=1, source_target_pairs={{0,1},{1,0},{2,3},{3,2},{4,5},{5,4},{6,7},{7,6},{8,9},{9,8},{10,11... | collective-permute-start | bytes 196616 | tf_op jit(solution)/shard_map/ppermute | solution.py:75
  40.3 0.7 %collective-permute-start.22 = (bf16[4,32,128]{2,1,0:T(8,128)(2,1)S(1)}, bf16[4,32,128]{2,1,0:T(8,128)(2,1)S(1)}, u32[]{:S(2)}, u32[]{:S(2)}) collective-permute-start(bf16[4,32,128]{2,1,0:T(8,128)(2,1)S(1)} %get-tuple-element.128), channel_id=1, source_target_pairs={{0,24},{1,25},{2,26},{3,27},{4,28},{5,29},{6,30},{7,31},{8,16},{9,... | collective-permute-start | bytes 98312 | tf_op jit(solution)/shard_map/ppermute | solution.py:75
  41.5 2.4 %step.11 = (f32[105,32,128]{2,1,0:T(8,128)S(1)}, f32[105,32,128]{2,1,0:T(8,128)S(1)}, f32[105,32,128]{2,1,0:T(8,128)S(1)}, bf16[105,32,128]{2,1,0:T(8,128)(2,1)S(1)}) custom-call(s32[537]{0:T(1024)S(4)} %get-tuple-element.79.info_ref, f32[9]{0:T(128)S(4)} %get-tuple-element.80.coeff_ref, ...), custom_call_target="tpu_custom_call", output_to_operand_aliasing={{0}: (7, {}), {1}: (8, {}), {2}: (9, {}), {3}: (10, {})} | custom-call | flops 327155712 | bytes 1048576 | tf_op jit(solution)/shard_map/step/pallas_call | solution.py:343
  44.4 1.6 %collective-permute-start.24 = (bf16[8,32,128]{2,1,0:T(8,128)(2,1)S(1)}, bf16[8,32,128]{2,1,0:T(8,128)(2,1)S(1)}, u32[]{:S(2)}, u32[]{:S(2)}) collective-permute-start(bf16[8,32,128]{2,1,0:T(8,128)(2,1)S(1)} %get-tuple-element.130), channel_id=1, source_target_pairs={{0,1},{1,0},{2,3},{3,2},{4,5},{5,4},{6,7},{7,6},{8,9},{9,8},{10,11... | collective-permute-start | bytes 196616 | tf_op jit(solution)/shard_map/ppermute | solution.py:75
  47.7 2.4 %step.12 = (f32[105,32,128]{2,1,0:T(8,128)S(1)}, f32[105,32,128]{2,1,0:T(8,128)S(1)}, f32[105,32,128]{2,1,0:T(8,128)S(1)}, bf16[105,32,128]{2,1,0:T(8,128)(2,1)S(1)}) custom-call(s32[537]{0:T(1024)S(4)} %get-tuple-element.79.info_ref, f32[9]{0:T(128)S(4)} %get-tuple-element.80.coeff_ref, ...), custom_call_target="tpu_custom_call", output_to_operand_aliasing={{0}: (7, {}), {1}: (8, {}), {2}: (9, {}), {3}: (10, {})} | custom-call | flops 327155712 | bytes 1048576 | tf_op jit(solution)/shard_map/step/pallas_call | solution.py:343
  50.5 2.8 %collective-permute-start.28 = (bf16[8,32,128]{2,1,0:T(8,128)(2,1)S(1)}, bf16[8,32,128]{2,1,0:T(8,128)(2,1)S(1)}, u32[]{:S(2)}, u32[]{:S(2)}) collective-permute-start(bf16[8,32,128]{2,1,0:T(8,128)(2,1)S(1)} %get-tuple-element.144), channel_id=1, source_target_pairs={{0,1},{1,0},{2,3},{3,2},{4,5},{5,4},{6,7},{7,6},{8,9},{9,8},{10,11... | collective-permute-start | bytes 196616 | tf_op jit(solution)/shard_map/ppermute | solution.py:75
  55.1 2.4 %step.13 = (f32[105,32,128]{2,1,0:T(8,128)S(1)}, f32[105,32,128]{2,1,0:T(8,128)S(1)}, f32[105,32,128]{2,1,0:T(8,128)S(1)}, bf16[105,32,128]{2,1,0:T(8,128)(2,1)S(1)}) custom-call(s32[537]{0:T(1024)S(4)} %get-tuple-element.79.info_ref, f32[9]{0:T(128)S(4)} %get-tuple-element.80.coeff_ref, ...), custom_call_target="tpu_custom_call", output_to_operand_aliasing={{0}: (7, {}), {1}: (8, {}), {2}: (9, {}), {3}: (10, {})} | custom-call | flops 327155712 | bytes 1048576 | tf_op jit(solution)/shard_map/step/pallas_call | solution.py:343
  57.5 1.5 %final.1 = (f32[32,13312]{1,0:T(8,128)}, f32[105,32,128]{2,1,0:T(8,128)S(1)}) custom-call(s32[537]{0:T(1024)S(4)} %get-tuple-element.79.info_ref, f32[9]{0:T(128)S(4)} %get-tuple-element.80.coeff_ref, bf16[312,128,128]{2,1,0:T(8,128)(2,1)S(1)} %get-tuple-element.81.bt_ref, ...), custom_call_target="tpu_custom_call", output_to_operand_aliasing={{1}: (3, {})} | custom-call | tf_op jit(solution)/shard_map/final/pallas_call | solution.py:356
  (64 shorter events, 12.4 us)
Async XLA Ops:
  1.6 8.1 %collective-permute-start = (bf16[8,32,128]{2,1,0:T(8,128)(2,1)S(1)}, bf16[8,32,128]{2,1,0:T(8,128)(2,1)S(1)}, u32[]{:S(2)}, u32[]{:S(2)}) collective-permute-start(bf16[8,32,128]{2,1,0:T(8,128)(2,1)S(1)} %get-tuple-element.83), channel_id=1, source_target_pairs={{0,1},{1,0},{2,3},{3,2},{4,5},{5,4},{6,7},{7,6},{8,9},{9,8},{10,11... | collective-permute-start | bytes 196616 | tf_op jit(solution)/shard_map/ppermute | solution.py:75
  3.7 6.0 %collective-permute-start.1 = (bf16[8,32,128]{2,1,0:T(8,128)(2,1)S(1)}, bf16[8,32,128]{2,1,0:T(8,128)(2,1)S(1)}, u32[]{:S(2)}, u32[]{:S(2)}) collective-permute-start(bf16[8,32,128]{2,1,0:T(8,128)(2,1)S(1)} %get-tuple-element.84), channel_id=1, source_target_pairs={{0,8},{1,2},{2,1},{3,4},{4,3},{5,6},{6,5},{7,15},{8,0},{9,10},{10,... | collective-permute-start | bytes 196616 | tf_op jit(solution)/shard_map/ppermute | solution.py:75
  4.7 5.0 %collective-permute-start.2 = (bf16[4,32,128]{2,1,0:T(8,128)(2,1)S(1)}, bf16[4,32,128]{2,1,0:T(8,128)(2,1)S(1)}, u32[]{:S(2)}, u32[]{:S(2)}) collective-permute-start(bf16[4,32,128]{2,1,0:T(8,128)(2,1)S(1)} %get-tuple-element.85), channel_id=1, source_target_pairs={{0,24},{1,25},{2,26},{3,27},{4,28},{5,29},{6,30},{7,31},{8,16},{9,... | collective-permute-start | bytes 98312 | tf_op jit(solution)/shard_map/ppermute | solution.py:75
  5.8 3.9 %collective-permute-start.3 = (bf16[4,32,128]{2,1,0:T(8,128)(2,1)S(1)}, bf16[4,32,128]{2,1,0:T(8,128)(2,1)S(1)}, u32[]{:S(2)}, u32[]{:S(2)}) collective-permute-start(bf16[4,32,128]{2,1,0:T(8,128)(2,1)S(1)} %get-tuple-element.86), channel_id=1, source_target_pairs={{0,8},{1,9},{2,10},{3,11},{4,12},{5,13},{6,14},{7,15},{8,0},{9,1},... | collective-permute-start | bytes 98312 | tf_op jit(solution)/shard_map/ppermute | solution.py:75
  10.0 6.4 %collective-permute-start.4 = (bf16[8,32,128]{2,1,0:T(8,128)(2,1)S(1)}, bf16[8,32,128]{2,1,0:T(8,128)(2,1)S(1)}, u32[]{:S(2)}, u32[]{:S(2)}) collective-permute-start(bf16[8,32,128]{2,1,0:T(8,128)(2,1)S(1)} %get-tuple-element.90), channel_id=1, source_target_pairs={{0,1},{1,0},{2,3},{3,2},{4,5},{5,4},{6,7},{7,6},{8,9},{9,8},{10,11... | collective-permute-start | bytes 196616 | tf_op jit(solution)/shard_map/ppermute | solution.py:75
  12.4 4.1 %collective-permute-start.5 = (bf16[8,32,128]{2,1,0:T(8,128)(2,1)S(1)}, bf16[8,32,128]{2,1,0:T(8,128)(2,1)S(1)}, u32[]{:S(2)}, u32[]{:S(2)}) collective-permute-start(bf16[8,32,128]{2,1,0:T(8,128)(2,1)S(1)} %get-tuple-element.91), channel_id=1, source_target_pairs={{0,8},{1,2},{2,1},{3,4},{4,3},{5,6},{6,5},{7,15},{8,0},{9,10},{10,... | collective-permute-start | bytes 196616 | tf_op jit(solution)/shard_map/ppermute | solution.py:75
  16.8 6.9 %collective-permute-start.8 = (bf16[8,32,128]{2,1,0:T(8,128)(2,1)S(1)}, bf16[8,32,128]{2,1,0:T(8,128)(2,1)S(1)}, u32[]{:S(2)}, u32[]{:S(2)}) collective-permute-start(bf16[8,32,128]{2,1,0:T(8,128)(2,1)S(1)} %get-tuple-element.94), channel_id=1, source_target_pairs={{0,1},{1,0},{2,3},{3,2},{4,5},{5,4},{6,7},{7,6},{8,9},{9,8},{10,11... | collective-permute-start | bytes 196616 | tf_op jit(solution)/shard_map/ppermute | solution.py:75
  19.0 4.7 %collective-permute-start.9 = (bf16[8,32,128]{2,1,0:T(8,128)(2,1)S(1)}, bf16[8,32,128]{2,1,0:T(8,128)(2,1)S(1)}, u32[]{:S(2)}, u32[]{:S(2)}) collective-permute-start(bf16[8,32,128]{2,1,0:T(8,128)(2,1)S(1)} %get-tuple-element.95), channel_id=1, source_target_pairs={{0,8},{1,2},{2,1},{3,4},{4,3},{5,6},{6,5},{7,15},{8,0},{9,10},{10,... | collective-permute-start | bytes 196616 | tf_op jit(solution)/shard_map/ppermute | solution.py:75
  19.9 3.8 %collective-permute-start.10 = (bf16[4,32,128]{2,1,0:T(8,128)(2,1)S(1)}, bf16[4,32,128]{2,1,0:T(8,128)(2,1)S(1)}, u32[]{:S(2)}, u32[]{:S(2)}) collective-permute-start(bf16[4,32,128]{2,1,0:T(8,128)(2,1)S(1)} %get-tuple-element.96), channel_id=1, source_target_pairs={{0,24},{1,25},{2,26},{3,27},{4,28},{5,29},{6,30},{7,31},{8,16},{9,... | collective-permute-start | bytes 98312 | tf_op jit(solution)/shard_map/ppermute | solution.py:75
  24.1 6.4 %collective-permute-start.12 = (bf16[8,32,128]{2,1,0:T(8,128)(2,1)S(1)}, bf16[8,32,128]{2,1,0:T(8,128)(2,1)S(1)}, u32[]{:S(2)}, u32[]{:S(2)}) collective-permute-start(bf16[8,32,128]{2,1,0:T(8,128)(2,1)S(1)} %get-tuple-element.108), channel_id=1, source_target_pairs={{0,1},{1,0},{2,3},{3,2},{4,5},{5,4},{6,7},{7,6},{8,9},{9,8},{10,11... | collective-permute-start | bytes 196616 | tf_op jit(solution)/shard_map/ppermute | solution.py:75
  26.4 4.1 %collective-permute-start.13 = (bf16[8,32,128]{2,1,0:T(8,128)(2,1)S(1)}, bf16[8,32,128]{2,1,0:T(8,128)(2,1)S(1)}, u32[]{:S(2)}, u32[]{:S(2)}) collective-permute-start(bf16[8,32,128]{2,1,0:T(8,128)(2,1)S(1)} %get-tuple-element.109), channel_id=1, source_target_pairs={{0,8},{1,2},{2,1},{3,4},{4,3},{5,6},{6,5},{7,15},{8,0},{9,10},{10,... | collective-permute-start | bytes 196616 | tf_op jit(solution)/shard_map/ppermute | solution.py:75
  26.9 3.6 %collective-permute-start.14 = (bf16[4,32,128]{2,1,0:T(8,128)(2,1)S(1)}, bf16[4,32,128]{2,1,0:T(8,128)(2,1)S(1)}, u32[]{:S(2)}, u32[]{:S(2)}) collective-permute-start(bf16[4,32,128]{2,1,0:T(8,128)(2,1)S(1)} %get-tuple-element.110), channel_id=1, source_target_pairs={{0,24},{1,25},{2,26},{3,27},{4,28},{5,29},{6,30},{7,31},{8,16},{9,... | collective-permute-start | bytes 98312 | tf_op jit(solution)/shard_map/ppermute | solution.py:75
  30.9 5.7 %collective-permute-start.16 = (bf16[8,32,128]{2,1,0:T(8,128)(2,1)S(1)}, bf16[8,32,128]{2,1,0:T(8,128)(2,1)S(1)}, u32[]{:S(2)}, u32[]{:S(2)}) collective-permute-start(bf16[8,32,128]{2,1,0:T(8,128)(2,1)S(1)} %get-tuple-element.112), channel_id=1, source_target_pairs={{0,1},{1,0},{2,3},{3,2},{4,5},{5,4},{6,7},{7,6},{8,9},{9,8},{10,11... | collective-permute-start | bytes 196616 | tf_op jit(solution)/shard_map/ppermute | solution.py:75
  32.4 4.2 %collective-permute-start.17 = (bf16[8,32,128]{2,1,0:T(8,128)(2,1)S(1)}, bf16[8,32,128]{2,1,0:T(8,128)(2,1)S(1)}, u32[]{:S(2)}, u32[]{:S(2)}) collective-permute-start(bf16[8,32,128]{2,1,0:T(8,128)(2,1)S(1)} %get-tuple-element.113), channel_id=1, source_target_pairs={{0,8},{1,2},{2,1},{3,4},{4,3},{5,6},{6,5},{7,15},{8,0},{9,10},{10,... | collective-permute-start | bytes 196616 | tf_op jit(solution)/shard_map/ppermute | solution.py:75
  33.0 3.6 %collective-permute-start.18 = (bf16[4,32,128]{2,1,0:T(8,128)(2,1)S(1)}, bf16[4,32,128]{2,1,0:T(8,128)(2,1)S(1)}, u32[]{:S(2)}, u32[]{:S(2)}) collective-permute-start(bf16[4,32,128]{2,1,0:T(8,128)(2,1)S(1)} %get-tuple-element.114), channel_id=1, source_target_pairs={{0,24},{1,25},{2,26},{3,27},{4,28},{5,29},{6,30},{7,31},{8,16},{9,... | collective-permute-start | bytes 98312 | tf_op jit(solution)/shard_map/ppermute | solution.py:75
  36.9 7.0 %collective-permute-start.20 = (bf16[8,32,128]{2,1,0:T(8,128)(2,1)S(1)}, bf16[8,32,128]{2,1,0:T(8,128)(2,1)S(1)}, u32[]{:S(2)}, u32[]{:S(2)}) collective-permute-start(bf16[8,32,128]{2,1,0:T(8,128)(2,1)S(1)} %get-tuple-element.126), channel_id=1, source_target_pairs={{0,1},{1,0},{2,3},{3,2},{4,5},{5,4},{6,7},{7,6},{8,9},{9,8},{10,11... | collective-permute-start | bytes 196616 | tf_op jit(solution)/shard_map/ppermute | solution.py:75
  39.8 4.1 %collective-permute-start.21 = (bf16[8,32,128]{2,1,0:T(8,128)(2,1)S(1)}, bf16[8,32,128]{2,1,0:T(8,128)(2,1)S(1)}, u32[]{:S(2)}, u32[]{:S(2)}) collective-permute-start(bf16[8,32,128]{2,1,0:T(8,128)(2,1)S(1)} %get-tuple-element.127), channel_id=1, source_target_pairs={{0,8},{1,2},{2,1},{3,4},{4,3},{5,6},{6,5},{7,15},{8,0},{9,10},{10,... | collective-permute-start | bytes 196616 | tf_op jit(solution)/shard_map/ppermute | solution.py:75
  40.3 3.6 %collective-permute-start.22 = (bf16[4,32,128]{2,1,0:T(8,128)(2,1)S(1)}, bf16[4,32,128]{2,1,0:T(8,128)(2,1)S(1)}, u32[]{:S(2)}, u32[]{:S(2)}) collective-permute-start(bf16[4,32,128]{2,1,0:T(8,128)(2,1)S(1)} %get-tuple-element.128), channel_id=1, source_target_pairs={{0,24},{1,25},{2,26},{3,27},{4,28},{5,29},{6,30},{7,31},{8,16},{9,... | collective-permute-start | bytes 98312 | tf_op jit(solution)/shard_map/ppermute | solution.py:75
  44.4 5.7 %collective-permute-start.24 = (bf16[8,32,128]{2,1,0:T(8,128)(2,1)S(1)}, bf16[8,32,128]{2,1,0:T(8,128)(2,1)S(1)}, u32[]{:S(2)}, u32[]{:S(2)}) collective-permute-start(bf16[8,32,128]{2,1,0:T(8,128)(2,1)S(1)} %get-tuple-element.130), channel_id=1, source_target_pairs={{0,1},{1,0},{2,3},{3,2},{4,5},{5,4},{6,7},{7,6},{8,9},{9,8},{10,11... | collective-permute-start | bytes 196616 | tf_op jit(solution)/shard_map/ppermute | solution.py:75
  46.0 4.1 %collective-permute-start.25 = (bf16[8,32,128]{2,1,0:T(8,128)(2,1)S(1)}, bf16[8,32,128]{2,1,0:T(8,128)(2,1)S(1)}, u32[]{:S(2)}, u32[]{:S(2)}) collective-permute-start(bf16[8,32,128]{2,1,0:T(8,128)(2,1)S(1)} %get-tuple-element.131), channel_id=1, source_target_pairs={{0,8},{1,2},{2,1},{3,4},{4,3},{5,6},{6,5},{7,15},{8,0},{9,10},{10,... | collective-permute-start | bytes 196616 | tf_op jit(solution)/shard_map/ppermute | solution.py:75
  46.5 3.6 %collective-permute-start.26 = (bf16[4,32,128]{2,1,0:T(8,128)(2,1)S(1)}, bf16[4,32,128]{2,1,0:T(8,128)(2,1)S(1)}, u32[]{:S(2)}, u32[]{:S(2)}) collective-permute-start(bf16[4,32,128]{2,1,0:T(8,128)(2,1)S(1)} %get-tuple-element.132), channel_id=1, source_target_pairs={{0,24},{1,25},{2,26},{3,27},{4,28},{5,29},{6,30},{7,31},{8,16},{9,... | collective-permute-start | bytes 98312 | tf_op jit(solution)/shard_map/ppermute | solution.py:75
  50.5 7.0 %collective-permute-start.28 = (bf16[8,32,128]{2,1,0:T(8,128)(2,1)S(1)}, bf16[8,32,128]{2,1,0:T(8,128)(2,1)S(1)}, u32[]{:S(2)}, u32[]{:S(2)}) collective-permute-start(bf16[8,32,128]{2,1,0:T(8,128)(2,1)S(1)} %get-tuple-element.144), channel_id=1, source_target_pairs={{0,1},{1,0},{2,3},{3,2},{4,5},{5,4},{6,7},{7,6},{8,9},{9,8},{10,11... | collective-permute-start | bytes 196616 | tf_op jit(solution)/shard_map/ppermute | solution.py:75
  53.4 4.2 %collective-permute-start.29 = (bf16[8,32,128]{2,1,0:T(8,128)(2,1)S(1)}, bf16[8,32,128]{2,1,0:T(8,128)(2,1)S(1)}, u32[]{:S(2)}, u32[]{:S(2)}) collective-permute-start(bf16[8,32,128]{2,1,0:T(8,128)(2,1)S(1)} %get-tuple-element.145), channel_id=1, source_target_pairs={{0,8},{1,2},{2,1},{3,4},{4,3},{5,6},{6,5},{7,15},{8,0},{9,10},{10,... | collective-permute-start | bytes 196616 | tf_op jit(solution)/shard_map/ppermute | solution.py:75
  53.9 3.6 %collective-permute-start.30 = (bf16[4,32,128]{2,1,0:T(8,128)(2,1)S(1)}, bf16[4,32,128]{2,1,0:T(8,128)(2,1)S(1)}, u32[]{:S(2)}, u32[]{:S(2)}) collective-permute-start(bf16[4,32,128]{2,1,0:T(8,128)(2,1)S(1)} %get-tuple-element.146), channel_id=1, source_target_pairs={{0,24},{1,25},{2,26},{3,27},{4,28},{5,29},{6,30},{7,31},{8,16},{9,... | collective-permute-start | bytes 98312 | tf_op jit(solution)/shard_map/ppermute | solution.py:75
  (11 other events, 43.0 us)
